TPU v7x, 32 devices: a whole 2x2x4 slice. The times are simulated.
32 devices in a mesh: scen: 4 (over y, x), fac: 8 (over z, core).
Axes of the slice: x: 2, y: 2, z: 4, core: 2. Of those that a mesh axis runs over, the one named last changes fastest.
Arguments:
- loadings: bfloat16 [8192, 1000], P('fac'), may hold values from -0.1875 to 0.1875
- reduced_shocks: bfloat16 [1000, 256], P(None, 'scen'), may hold values from -6 to 6
- sensitivity: bfloat16 [8192, 200], P('fac'), may hold values from -0.0625 to 0.0625
- cross_gamma: bfloat16 [16, 1024, 1024], P('fac'), may hold values from -0.005859375 to 0.005859375
- block_list: int32 [12, 3], replicated, may hold values from 0 to 199, as said below
- block_owner: int32 [12], replicated, may hold values from 0 to 7, as said below
- desk_owner: int32 [200], replicated, may hold values from 0 to 7, as said below
- buckets: int32 [8192], replicated, may hold values from 0 to 4
Outputs:
- desk_profit: float32 [208, 5, 256], P('fac', None, 'scen')
- shortfall: float32 [208, 5], P('fac')
- adjusted_es: float32 [208], P('fac')
Inputs may be any that keep to these rules, and one draw needn't show every extreme that they name: `block_list`: each row is (row block, column block, desk): block numbers below 8, desks below 200; the fac index holding the row block, and the one holding the column block, is at most two away from the block's owner. `block_owner`: no fac index owns more than 2 blocks; some index owns exactly 2. `desk_owner`: no fac index owns more than 26 desks; some index owns exactly 26.
All inputs are finite; a program needn't handle non-finite values.
Results may differ from a plain program's by a relative error of at most 0.0032.
Values may be sent and summed in bfloat16 or wider, within the bound.
A program may use at most 64 MiB of HBM per device.

v0:
```python
import jax
import jax.numpy as jnp
from jax import lax
from jax.sharding import PartitionSpec as P

BLK = 1024
HORIZONS = 5
CAP = 2


horizon_weights = (1.0, 1.0, 2.0, 2.0, 6.0)


def passed_along(value, axis, steps):
    count = lax.axis_size(axis)
    initial, last = (max(0, -steps), min(count, count - steps))
    return lax.ppermute(value, axis, [(source, source + steps) for source in range(initial, last)])


def owner_ranks(owners):
    position = jnp.arange(owners.shape[0], dtype=jnp.int32)
    same_owner = owners[:, None] == owners[None, :]
    earlier = position[None, :] < position[:, None]
    return jnp.sum((same_owner & earlier).astype(jnp.int32), axis=1)


def apply_masks(shocks, bucket_ids):
    horizon = jnp.arange(HORIZONS, dtype=jnp.int32)
    keeps_factor = bucket_ids[:, None] >= horizon[None, :]
    masked = jnp.where(keeps_factor[:, :, None], shocks[:, None, :], jnp.zeros((), jnp.bfloat16))
    return masked.reshape(shocks.shape[0], HORIZONS * shocks.shape[1])


def local(
    loadings, reduced_shocks, sensitivity, cross_gamma, block_list, block_owner, desk_owner, buckets
):
    device = lax.axis_index("fac")
    fac_count = lax.axis_size("fac")
    f_dev = loadings.shape[0]
    s_dev = reduced_shocks.shape[1]
    desks = sensitivity.shape[1]
    blocks = block_owner.shape[0]
    shocks = jnp.dot(loadings, reduced_shocks, preferred_element_type=jnp.float32).astype(
        jnp.bfloat16
    )
    own_buckets = lax.dynamic_slice_in_dim(buckets, device * f_dev, f_dev)
    masked = apply_masks(shocks, own_buckets)
    partial_value = lax.dot_general(
        sensitivity, masked, (((0,), (0,)), ((), ())), preferred_element_type=jnp.float32
    )
    pieces = {}
    for distance in (2, 1, -1, -2):
        pieces[distance] = passed_along(masked, "fac", distance)
    window = jnp.concatenate([pieces[2], pieces[1], masked, pieces[-1], pieces[-2]], axis=0)
    row_base = (device - 2) * f_dev
    block_rank = owner_ranks(block_owner)
    owned = block_owner == device
    slot_ids = jnp.arange(CAP, dtype=jnp.int32)
    picked = owned[None, :] & (block_rank[None, :] == slot_ids[:, None])
    slot_block = jnp.sum(jnp.where(picked, jnp.arange(blocks, dtype=jnp.int32)[None, :], 0), axis=1)
    live_blocks = jnp.sum(owned.astype(jnp.int32))
    desk_ids = jnp.arange(desks, dtype=jnp.int32)

    def add_block(slot_index, running):
        block_entry = block_list[slot_block[slot_index]]
        matrix = lax.dynamic_index_in_dim(cross_gamma, slot_index, 0, keepdims=False)
        row_part = lax.dynamic_slice_in_dim(window, block_entry[0] * BLK - row_base, BLK, 0)
        col_part = lax.dynamic_slice_in_dim(window, block_entry[1] * BLK - row_base, BLK, 0)
        product = jnp.dot(matrix, col_part, preferred_element_type=jnp.float32)
        quad_term = 0.5 * jnp.sum(row_part.astype(jnp.float32) * product, axis=0)
        return running + jnp.where(
            (desk_ids == block_entry[2])[:, None], quad_term[None, :], jnp.zeros((), jnp.float32)
        )

    partial_value = lax.fori_loop(0, live_blocks, add_block, partial_value)
    desk_dev = (desks + fac_count - 1) // fac_count + 1
    desk_slot = desk_owner * desk_dev + owner_ranks(desk_owner)
    placement = (
        desk_slot[:, None] == jnp.arange(desk_dev * fac_count, dtype=jnp.int32)[None, :]
    ).astype(jnp.float32)
    desk_terms = lax.dot_general(
        placement,
        partial_value,
        (((0,), (0,)), ((), ())),
        precision=lax.Precision.HIGHEST,
        preferred_element_type=jnp.float32,
    )
    owned_rows = lax.psum_scatter(desk_terms, "fac", scatter_dimension=0, tiled=True)
    profit = owned_rows.reshape(desk_dev, HORIZONS, s_dev)
    tail_count = (s_dev * lax.axis_size("scen") * 25 + 999) // 1000
    all_scenarios = lax.all_gather(profit, "scen", axis=2, tiled=True)
    worst_losses = lax.top_k(-all_scenarios, tail_count)[0]
    shortfall = jnp.mean(worst_losses, axis=2)
    weights = jnp.array(horizon_weights, jnp.float32)
    adjusted = jnp.sqrt(jnp.sum(weights[None, :] * shortfall * shortfall, axis=1) + 1e-06)
    return (profit, shortfall, adjusted)


def solution(mesh):
    return jax.shard_map(
        local,
        mesh=mesh,
        in_specs=(
            P("fac", None),
            P(None, "scen"),
            P("fac", None),
            P("fac", None, None),
            P(),
            P(),
            P(),
            P(),
        ),
        out_specs=(P("fac", None, "scen"), P("fac", None), P("fac")),
        check_vma=False,
    )
```

profile of v0, /device:TPU:0, one launch (start us, length us, event | category | flops | bytes accessed | tf_op | source)
XLA Modules:
  0.0 134.2 jit_solution(10274268695481209215)
XLA Ops:
  0.6 0.0 copy-start
  0.6 0.0 copy-start.1
  0.7 0.0 copy-start.4
  0.7 0.0 copy-start.7
  0.7 0.8 dynamic_slice.19
  1.5 0.7 copy-done
  2.2 1.4 %convolution_convert_fusion = bf16[1024,64]{0,1:T(8,128)(2,1)S(1)} fusion(bf16[1024,1000]{0,1:T(8,128)(2,1)S(1)} %copy-done, bf16[1000,64]{0,1:T(8,128)(2,1)} %param.12), kind=kOutput, calls=%fused_computation.13 | convolution fusion | flops 131137536 | bytes 2307072 | tf_op jit(solution)/shard_map/dot_general | solution.py:43
  3.6 0.1 broadcast_select_fusion
  3.7 5.8 %collective-permute-start = (bf16[1024,320]{0,1:T(8,128)(2,1)S(1)}, bf16[1024,320]{0,1:T(8,128)(2,1)}, u32[]{:S(2)}, u32[]{:S(2)}) collective-permute-start(bf16[1024,320]{0,1:T(8,128)(2,1)S(1)} %bitcast.32), channel_id=1, source_target_pairs={{0,2},{1,3},{2,4},{3,5},{4,6},{5,7},{8,10},{9,11},{10,12},{11,13},... | collective-permute-start | bytes 1966088 | tf_op jit(solution)/shard_map/ppermute | solution.py:17
  9.4 2.3 %collective-permute-start.1 = (bf16[1024,320]{0,1:T(8,128)(2,1)S(1)}, bf16[1024,320]{0,1:T(8,128)(2,1)}, u32[]{:S(2)}, u32[]{:S(2)}) collective-permute-start(bf16[1024,320]{0,1:T(8,128)(2,1)S(1)} %bitcast.33), channel_id=1, source_target_pairs={{0,1},{1,2},{2,3},{3,4},{4,5},{5,6},{6,7},{8,9},{9,10},{10,11},{11... | collective-permute-start | bytes 1966088 | tf_op jit(solution)/shard_map/ppermute | solution.py:17
  11.8 1.3 collective-permute-start.2
  13.0 1.3 collective-permute-start.3
  14.3 0.0 copy-done.1
  14.4 0.4 convolution_bitcast_fusion
  14.8 0.0 copy-done.4
  14.8 0.2 convert_reduce_fusion
  15.0 0.0 copy-done.7
  15.0 0.6 convert_reduce_fusion.2
  15.6 0.2 convert_reduce_fusion.1
  15.8 0.1 fusion.18
  15.9 0.0 copy-start.3
  16.0 7.8 %collective-permute-done = bf16[1024,320]{0,1:T(8,128)(2,1)} collective-permute-done((bf16[1024,320]{0,1:T(8,128)(2,1)S(1)}, bf16[1024,320]{0,1:T(8,128)(2,1)}, u32[]{:S(2)}, u32[]{:S(2)}) %collective-permute-start) | collective-permute-done | bytes 655392 | tf_op jit(solution)/shard_map/ppermute | solution.py:17
  23.7 1.1 constant_dynamic-update-slice_fusion.4
  24.9 0.0 collective-permute-done.1
  24.9 1.1 constant_dynamic-update-slice_fusion.3
  26.1 0.0 collective-permute-done.2
  26.1 1.1 constant_dynamic-update-slice_fusion.1
  27.2 11.2 %collective-permute-done.3 = bf16[1024,320]{0,1:T(8,128)(2,1)} collective-permute-done((bf16[1024,320]{0,1:T(8,128)(2,1)S(1)}, bf16[1024,320]{0,1:T(8,128)(2,1)}, u32[]{:S(2)}, u32[]{:S(2)}) %collective-permute-start.3) | collective-permute-done | bytes 655392 | tf_op jit(solution)/shard_map/ppermute | solution.py:17
  38.5 1.1 constant_dynamic-update-slice_fusion
  39.6 0.0 copy-start.2
  39.6 1.7 %copy-done.2 = bf16[5120,320]{0,1:T(8,128)(2,1)} copy-done((bf16[5120,320]{0,1:T(8,128)(2,1)}, bf16[5120,320]{0,1:T(8,128)(2,1)S(1)}, u32[]{:S(2)}) %copy-start.2) | copy-done | bytes 3276824
  41.3 0.0 copy-done.3
  41.3 0.0 copy-start.6
  41.3 9.2 %while.11 = (s32[]{:T(128)}, f32[200,320]{1,0:T(8,128)S(1)}, s32[]{:T(128)}, s32[2]{0:T(128)S(1)}, s32[12,3]{0,1:T(4,128)S(1)}, /*index=5*/s32[]{:T(128)}, bf16[...) while((s32[]{:T(128)}, f32[200,320]{1,0:T(8,128)S(1)}, ...), condition=%wide.region_6.7_spmd.clone, body=%wide.region_4.6_spmd.clone.sunk | while | flops 672199872 | bytes 3925789 | solution.py:75
  42.0 0.6 dynamic_slice.46
  44.2 0.1 constant_dynamic-slice_fusion.3
  44.3 0.6 fusion.31
  46.2 2.9 %fusion.32 = f32[320]{0:T(512)S(1)} fusion(bf16[2,1024,1024]{2,1,0:T(8,128)(2,1)} %get-tuple-element.210, s32[]{:T(128)S(6)} %select_n.53, bf16[5120,320]{0,1:T(8,128)(2,1)} %get-tuple-element.209, s32[]{:T(128)S(6)} %select_n.55, s32[]{:T(128)S(6)} %select_n.56), kind=kOutput, calls=%fused_computation.5.clone.1 | convolution fusion | flops 672071360 | bytes 3409164 | tf_op jit(solution)/shard_map/while/body/dot_general | solution.py:69
  49.1 0.6 iota_compare_fusion.7
  49.7 0.1 select_add_fusion.2
  50.5 0.0 copy-start.5
  50.5 0.5 fusion.15
  51.0 21.5 %fusion.2 = f32[32,320]{1,0:T(8,128)S(1)} fusion(f32[208,320]{1,0:T(8,128)S(1)} %fusion.15), kind=kCustom, calls=%all-reduce-scatter | all-reduce-scatter fusion | flops 81921 | bytes 307712
  72.5 1.5 %collective-permute-start.4 = (f32[32,320]{1,0:T(8,128)S(1)}, f32[32,320]{1,0:T(8,128)S(1)}, u32[]{:S(2)}, u32[]{:S(2)}) collective-permute-start(f32[32,320]{1,0:T(8,128)S(1)} %fusion.2), channel_id=1, source_target_pairs={{0,1},{1,2},{2,3},{3,4},{4,5},{5,6},{6,7},{8,9},{9,10},{10,11},{11... | collective-permute-start | bytes 122888
  74.1 3.6 %collective-permute-start.5 = (f32[10,320]{1,0:T(8,128)S(1)}, f32[10,320]{1,0:T(8,128)S(1)}, u32[]{:S(2)}, u32[]{:S(2)}) collective-permute-start(f32[10,320]{1,0:T(8,128)S(1)} %slice.16), channel_id=1, source_target_pairs={{0,2},{1,3},{2,4},{3,5},{4,6},{5,7},{8,10},{9,11},{10,12},{11,13},... | collective-permute-start | bytes 38408
  77.7 0.0 copy-done.6
  77.7 0.6 dynamic-slice.4
  78.9 0.3 collective-permute-done.5
  79.2 0.0 collective-permute-done.4
  79.2 0.3 concatenate.4
  79.5 0.1 reshape.60
  79.6 0.2 copy.27
  79.8 0.6 copy.30
  80.4 13.1 %all_gather.3 = f32[26,5,256]{0,1,2:T(8,128)S(1)} all-gather(f32[26,5,64]{0,1,2:T(8,128)S(1)} %copy.27), channel_id=1, replica_groups=mesh['scen'=4,'fac'=8] {'scen'}, dimensions={2}, use_global_device_ids=true | all-gather | bytes 166400 | tf_op jit(solution)/shard_map/all_gather | solution.py:91
  93.5 0.3 copy.28
  93.8 0.1 copy.29
  93.9 38.9 %sort_prefixfusion = f32[26,5,7]{2,1,0:T(8,128)S(1)} fusion(f32[26,5,256]{2,1,0:T(8,128)S(1)} %copy.29), kind=kCustom, calls=%top_k.9.sort_prefix | custom fusion | flops 532480 | bytes 136760 | tf_op jit(solution)/shard_map/top_k | solution.py:92
  132.7 0.1 reduce_sum.67
  132.8 0.0 copy-done.5
  132.9 0.1 multiply_reduce_fusion
  133.0 0.7 copy.31
  133.6 0.5 add_sqrt_fusion
  (7 shorter events, 0.1 us)
Async XLA Ops:
  0.6 1.6 %copy-start = (bf16[1024,1000]{0,1:T(8,128)(2,1)S(1)}, bf16[1024,1000]{0,1:T(8,128)(2,1)}, u32[]{:S(2)}) copy-start(bf16[1024,1000]{0,1:T(8,128)(2,1)} %param.11) | copy-start | bytes 6144004
  0.6 13.7 %copy-start.1 = (bf16[1024,200]{0,1:T(8,128)(2,1)S(1)}, bf16[1024,200]{0,1:T(8,128)(2,1)}, u32[]{:S(2)}) copy-start(bf16[1024,200]{0,1:T(8,128)(2,1)} %param.13) | copy-start | bytes 1228804
  0.7 14.1 %copy-start.4 = (s32[200]{0:T(256)S(1)}, s32[200]{0:T(256)}, u32[]{:S(2)}) copy-start(s32[200]{0:T(256)} %param.17) | copy-start | bytes 2404
  0.7 14.3 %copy-start.7 = (s32[12]{0:T(128)S(1)}, s32[12]{0:T(128)}, u32[]{:S(2)}) copy-start(s32[12]{0:T(128)} %param.16) | copy-start | bytes 148
  3.7 20.1 %collective-permute-start = (bf16[1024,320]{0,1:T(8,128)(2,1)S(1)}, bf16[1024,320]{0,1:T(8,128)(2,1)}, u32[]{:S(2)}, u32[]{:S(2)}) collective-permute-start(bf16[1024,320]{0,1:T(8,128)(2,1)S(1)} %bitcast.32), channel_id=1, source_target_pairs={{0,2},{1,3},{2,4},{3,5},{4,6},{5,7},{8,10},{9,11},{10,12},{11,13},... | collective-permute-start | bytes 1966088 | tf_op jit(solution)/shard_map/ppermute | solution.py:17
  9.4 15.4 %collective-permute-start.1 = (bf16[1024,320]{0,1:T(8,128)(2,1)S(1)}, bf16[1024,320]{0,1:T(8,128)(2,1)}, u32[]{:S(2)}, u32[]{:S(2)}) collective-permute-start(bf16[1024,320]{0,1:T(8,128)(2,1)S(1)} %bitcast.33), channel_id=1, source_target_pairs={{0,1},{1,2},{2,3},{3,4},{4,5},{5,6},{6,7},{8,9},{9,10},{10,11},{11... | collective-permute-start | bytes 1966088 | tf_op jit(solution)/shard_map/ppermute | solution.py:17
  11.8 14.3 %collective-permute-start.2 = (bf16[1024,320]{0,1:T(8,128)(2,1)S(1)}, bf16[1024,320]{0,1:T(8,128)(2,1)}, u32[]{:S(2)}, u32[]{:S(2)}) collective-permute-start(bf16[1024,320]{0,1:T(8,128)(2,1)S(1)} %bitcast.34), channel_id=1, source_target_pairs={{1,0},{2,1},{3,2},{4,3},{5,4},{6,5},{7,6},{9,8},{10,9},{11,10},{12... | collective-permute-start | bytes 1966088 | tf_op jit(solution)/shard_map/ppermute | solution.py:17
  13.0 25.4 %collective-permute-start.3 = (bf16[1024,320]{0,1:T(8,128)(2,1)S(1)}, bf16[1024,320]{0,1:T(8,128)(2,1)}, u32[]{:S(2)}, u32[]{:S(2)}) collective-permute-start(bf16[1024,320]{0,1:T(8,128)(2,1)S(1)} %bitcast.35), channel_id=1, source_target_pairs={{2,0},{3,1},{4,2},{5,3},{6,4},{7,5},{10,8},{11,9},{12,10},{13,11},... | collective-permute-start | bytes 1966088 | tf_op jit(solution)/shard_map/ppermute | solution.py:17
  15.9 25.3 %copy-start.3 = (s32[12,3]{0,1:T(4,128)S(1)}, s32[12,3]{0,1:T(4,128)}, u32[]{:S(2)}) copy-start(s32[12,3]{0,1:T(4,128)} %param.15) | copy-start | bytes 436
  39.6 1.7 %copy-start.2 = (bf16[5120,320]{0,1:T(8,128)(2,1)}, bf16[5120,320]{0,1:T(8,128)(2,1)S(1)}, u32[]{:S(2)}) copy-start(bf16[5120,320]{0,1:T(8,128)(2,1)S(1)} %constant_dynamic-update-slice_fusion) | copy-start | bytes 9830404
  41.3 36.4 %copy-start.6 = (u32[32]{0:T(128)S(1)}, u32[32]{0:T(128)}, u32[]{:S(2)}) copy-start(u32[32]{0:T(128)} %constant.60) | copy-start | bytes 388
  50.5 82.4 %copy-start.5 = (f32[5]{0:T(128)S(1)}, f32[5]{0:T(128)}, u32[]{:S(2)}) copy-start(f32[5]{0:T(128)} %constant.57) | copy-start | bytes 64
  72.5 6.7 %collective-permute-start.4 = (f32[32,320]{1,0:T(8,128)S(1)}, f32[32,320]{1,0:T(8,128)S(1)}, u32[]{:S(2)}, u32[]{:S(2)}) collective-permute-start(f32[32,320]{1,0:T(8,128)S(1)} %fusion.2), channel_id=1, source_target_pairs={{0,1},{1,2},{2,3},{3,4},{4,5},{5,6},{6,7},{8,9},{9,10},{10,11},{11... | collective-permute-start | bytes 122888
  74.1 5.1 %collective-permute-start.5 = (f32[10,320]{1,0:T(8,128)S(1)}, f32[10,320]{1,0:T(8,128)S(1)}, u32[]{:S(2)}, u32[]{:S(2)}) collective-permute-start(f32[10,320]{1,0:T(8,128)S(1)} %slice.16), channel_id=1, source_target_pairs={{0,2},{1,3},{2,4},{3,5},{4,6},{5,7},{8,10},{9,11},{10,12},{11,13},... | collective-permute-start | bytes 38408
where the time goes:
time: 135 us; the launch traced here: 134 us
  other arithmetic  41.5 us (31%)
  blocking collectives  34.6 us (26%)
  waiting for transfers between devices  19.3 us (14%)
  starting transfers between devices  15.8 us (12%)
  local copies, waits for them, and re-layouts  11.9 us (9%)
  matrix products  5.26 us (4%)
  loops' own time  4.32 us (3%)
  between operations  1.58 us (1%)
    top_k x1, other arithmetic, local(): worst_losses = lax.top_k(-all_scenarios, tail_count)[0]  38.9 us
    unnamed x1, blocking collectives  21.5 us
    ppermute x4, waiting for transfers between devices, passed_along(): lax.ppermute(value, axis, [(source, source + steps) for source in range(i...  19 us
    all_gather x1, blocking collectives, local(): all_scenarios = lax.all_gather(profit, 'scen', axis=2, tiled=True)  13.1 us
    ppermute x4, starting transfers between devices, passed_along(): lax.ppermute(value, axis, [(source, source + steps) for source in range(i...  10.7 us
    unnamed x26, local copies, waits for them, and re-layouts  8.07 us
    unnamed x2, starting transfers between devices  5.12 us
    another operation x1, loops' own time, local(): partial_value = lax.fori_loop(0, live_blocks, add_block, partial_value)  4.32 us
  transfers between devices with their start and end apart: 6, of which 3 were waited for; matrix products, arithmetic and copies ran while one was open for 4% of the time, Pallas kernels for 0%

commit v1 on v0

v1 whole, which is shorter than its diff:
```python
import functools

import jax
import jax.numpy as jnp
from jax import lax
from jax.experimental import pallas as pl
from jax.experimental.pallas import tpu as pltpu
from jax.sharding import PartitionSpec as P

HORIZONS = 5
CAP = 2
REACH = 2
WINDOW = 2 * REACH + 1
GROUP = 32
GROWS = 8
LIST = 8
MESH = pl.DeviceIdType.MESH
F32 = jnp.float32
BF16 = jnp.bfloat16

horizon_weights = (1.0, 1.0, 2.0, 2.0, 6.0)


def dot_nt(a, b):
    return lax.dot_general(a, b, (((1,), (1,)), ((), ())), preferred_element_type=F32)


def one_hot(condition):
    return jnp.where(condition, 1.0, 0.0).astype(BF16)


def exchange(items, i, j):
    high, low = jnp.maximum(items[i], items[j]), jnp.minimum(items[i], items[j])
    items[i], items[j] = high, low


SORT8 = (
    (0, 1), (2, 3), (4, 5), (6, 7), (0, 2), (1, 3), (4, 6), (5, 7), (1, 2), (5, 6),
    (0, 4), (1, 5), (2, 6), (3, 7), (2, 4), (3, 5), (1, 2), (3, 4), (5, 6),
)


def merge_sorted(first, second):
    items = [jnp.maximum(first[i], second[LIST - 1 - i]) for i in range(LIST)]
    for stride in (4, 2, 1):
        for i in range(LIST):
            if not i & stride:
                exchange(items, i, i + stride)
    return items


def tail_mean(losses, tail):
    items = [losses[8 * i : 8 * i + 8] for i in range(LIST)]
    for i, j in SORT8:
        exchange(items, i, j)
    for shift in (4, 2, 1):
        items = merge_sorted(items, [pltpu.roll(item, shift, 0) for item in items])
    items = merge_sorted(items, [pltpu.roll(item, 64, 1) for item in items])
    others = [pltpu.roll(item, 32, 1) for item in items]
    best = [jnp.maximum(items[i], others[tail - 1 - i]) for i in range(tail)]
    return sum(best[1:], best[0]) * (1.0 / tail)


def kernel(
    n, n_scen, tail, desk_dev,
    blist, bowner, desk_owner, buckets, loadings, reduced, sensitivity, gamma,
    profit_out, short_out, adjusted_out,
    lbuf, rbuf, sbuf, gbuf, win, masked, terms, pair_buf, totals, piece_out, piece_in,
    gam, scen_buf, rt_pad,
    local_sem, win_send, win_recv, pair_sem, piece_send, piece_recv, gam_send, gam_recv,
    scen_send, scen_recv,
):
    me = lax.axis_index("fac")
    sc = lax.axis_index("scen")
    nh = n // 2
    core, chip = lax.rem(me, 2), me // 2
    depth, s_dev = reduced.shape
    f_dev = loadings.shape[0]
    desks = sensitivity.shape[1]
    blocks = bowner.shape[0]
    hs = HORIZONS * s_dev

    local = [
        pltpu.make_async_copy(source, target, local_sem.at[i])
        for i, (source, target) in enumerate(
            ((reduced, rbuf), (loadings, lbuf), (sensitivity, sbuf), (gamma, gbuf))
        )
    ]
    for copy in local:
        copy.start()

    barrier = pltpu.get_barrier_semaphore()
    for step in range(1, n):
        pl.semaphore_signal(
            barrier, inc=1, device_id={"fac": lax.rem(me + step, n)}, device_id_type=MESH
        )
    for step in range(1, n_scen):
        pl.semaphore_signal(
            barrier, inc=1, device_id={"scen": lax.rem(sc + step, n_scen)}, device_id_type=MESH
        )

    owner_row = desk_owner[...]
    owns = one_hot(lax.broadcasted_iota(jnp.int32, (n, desks), 0) == owner_row)
    before = one_hot(
        lax.broadcasted_iota(jnp.int32, (desks, desks), 0)
        < lax.broadcasted_iota(jnp.int32, (desks, desks), 1)
    )
    earlier = jnp.dot(owns, before, preferred_element_type=F32)
    rank_row = jnp.sum(owns.astype(F32) * earlier, axis=0, keepdims=True).astype(jnp.int32)
    slot_row = ((owner_row & 1) * nh + (owner_row >> 1)) * GROUP + rank_row
    my_group = core * nh + chip

    bpad = (blocks + 15) // 16 * 16
    block_ids = lax.broadcasted_iota(jnp.int32, (bpad, 1), 0)

    def read_block(b, carry):
        count, live, rows, cols, owner_col, desk_col = carry
        owner = bowner[b]
        mine = owner == me
        live = tuple(
            jnp.where(mine & (count == k), 1, live[k]) for k in range(CAP)
        )
        rows = tuple(
            jnp.where(mine & (count == k), blist[b, 0], rows[k]) for k in range(CAP)
        )
        cols = tuple(
            jnp.where(mine & (count == k), blist[b, 1], cols[k]) for k in range(CAP)
        )
        owner_col = jnp.where(block_ids == b, owner, owner_col)
        desk_col = jnp.where(block_ids == b, blist[b, 2], desk_col)
        return count + jnp.where(mine, 1, 0), live, rows, cols, owner_col, desk_col

    empty = jnp.full((bpad, 1), -1, jnp.int32)
    zero = jnp.int32(0)
    _, live, rows, cols, owner_col, desk_col = lax.fori_loop(
        0, blocks, read_block, (zero, (zero,) * CAP, (me,) * CAP, (me,) * CAP, empty, empty)
    )
    block_owns = one_hot(owner_col == lax.broadcasted_iota(jnp.int32, (bpad, n), 1))
    above = one_hot(
        lax.broadcasted_iota(jnp.int32, (bpad, bpad), 0)
        > lax.broadcasted_iota(jnp.int32, (bpad, bpad), 1)
    )
    block_earlier = jnp.dot(above, block_owns, preferred_element_type=F32)
    block_rank = jnp.sum(
        block_owns.astype(F32) * block_earlier, axis=1, keepdims=True
    ).astype(jnp.int32)
    distance = me - owner_col
    distance = jnp.where(distance < 0, distance + n, distance)
    key = jnp.where(owner_col >= 0, distance * GROWS + block_rank, -1)
    key_hot = one_hot(key == lax.broadcasted_iota(jnp.int32, (bpad, n * GROWS), 1))
    desk_hot = one_hot(desk_col == lax.broadcasted_iota(jnp.int32, (bpad, desks), 1))
    my_desks = one_hot(
        lax.broadcasted_iota(jnp.int32, (GROUP, desks), 0) + my_group * GROUP == slot_row
    )
    gather_rows = jnp.dot(
        dot_nt(my_desks, desk_hot).astype(BF16), key_hot, preferred_element_type=F32
    )

    local[0].wait()
    rt_pad[...] = jnp.zeros_like(rt_pad)
    rt_pad[0:depth, 0:s_dev] = rbuf[...].astype(F32)
    reduced_t = jnp.transpose(rt_pad[...])[0:s_dev, 0:depth].astype(BF16)
    local[1].wait()
    win[REACH] = dot_nt(reduced_t, lbuf[...]).astype(BF16)

    pl.semaphore_wait(barrier, n - 1 + n_scen - 1)

    def window_copy(step):
        slot = REACH - step
        return pltpu.make_async_remote_copy(
            src_ref=win.at[REACH],
            dst_ref=win.at[slot],
            send_sem=win_send.at[slot],
            recv_sem=win_recv.at[slot],
            device_id={"fac": jnp.clip(me + step, 0, n - 1)},
            device_id_type=MESH,
        )

    steps = [step for step in range(-REACH, REACH + 1) if step]
    for step in steps:
        @pl.when((me + step >= 0) & (me + step < n))
        def _(step=step):
            window_copy(step).start()

    def keeps(index):
        return buckets[index]

    def masks(row, shape_rows):
        return [
            jnp.broadcast_to(jnp.where(row >= h, 1.0, 0.0), (shape_rows, f_dev))
            for h in range(HORIZONS)
        ]

    def fill_masked(shocks, row):
        shocks = shocks.astype(F32)
        for h in range(HORIZONS):
            masked[h * s_dev : (h + 1) * s_dev, :] = jnp.where(row >= h, shocks, 0.0).astype(BF16)

    fill_masked(win[REACH], keeps(me))
    local[2].wait()
    chunk = min(n * GROUP, 256)

    def add_terms(i, carry):
        start = pl.multiple_of(i * chunk, chunk)
        place = one_hot(
            lax.broadcasted_iota(jnp.int32, (chunk, desks), 0) + start == slot_row
        )
        placed = dot_nt(place, sbuf[...]).astype(BF16)
        terms[pl.ds(start, chunk), :] = dot_nt(placed, masked[...])
        return carry

    lax.fori_loop(0, n * GROUP // chunk, add_terms, 0)

    half = nh * GROUP
    pair = pltpu.make_async_remote_copy(
        src_ref=terms.at[pl.ds(pl.multiple_of((1 - core) * half, half), half)],
        dst_ref=pair_buf,
        send_sem=pair_sem.at[0],
        recv_sem=pair_sem.at[1],
        device_id={"fac": me + 1 - 2 * core},
        device_id_type=MESH,
    )
    pair.start()
    pair.wait_recv()
    for j in range(nh):
        start = pl.multiple_of(core * half + j * GROUP, GROUP)
        total = terms[pl.ds(start, GROUP), :] + pair_buf[j * GROUP : (j + 1) * GROUP, :]
        totals[j] = total
        piece_out[j] = total.astype(BF16)
    pieces = []
    for step in range(1, nh):
        target = lax.rem(chip + step, nh)
        copy = pltpu.make_async_remote_copy(
            src_ref=piece_out.at[target],
            dst_ref=piece_in.at[step],
            send_sem=piece_send.at[step],
            recv_sem=piece_recv.at[step],
            device_id={"fac": 2 * target + core},
            device_id_type=MESH,
        )
        copy.start()
        pieces.append(copy)

    for step in steps:
        @pl.when((me - step >= 0) & (me - step < n))
        def _(step=step):
            window_copy(step).wait_recv()
    local[3].wait()
    gam[0] = jnp.zeros((GROWS, hs), F32)
    for k in range(CAP):
        fill_masked(win[jnp.clip(cols[k] - me + REACH, 0, WINDOW - 1)], keeps(cols[k]))
        product = dot_nt(masked[...], gbuf[k])
        row_part = win[jnp.clip(rows[k] - me + REACH, 0, WINDOW - 1)].astype(F32)
        row_bucket = keeps(rows[k])
        folded = []
        for h in range(HORIZONS):
            part = jnp.where(row_bucket >= h, row_part, 0.0) * product[h * s_dev : (h + 1) * s_dev]
            folded.append(sum(part[:, i : i + 128] for i in range(0, f_dev, 128)))
        quad = jnp.sum(jnp.transpose(jnp.concatenate(folded, axis=0)), axis=0, keepdims=True)
        gam[0, k : k + 1, :] = quad * (0.5 * live[k].astype(F32))
    rows_out = []
    for step in range(1, n):
        copy = pltpu.make_async_remote_copy(
            src_ref=gam.at[0],
            dst_ref=gam.at[step],
            send_sem=gam_send.at[step],
            recv_sem=gam_recv.at[step],
            device_id={"fac": lax.rem(me + step, n)},
            device_id_type=MESH,
        )
        copy.start()
        rows_out.append(copy)

    own = totals[chip]
    for step, copy in enumerate(pieces, 1):
        copy.wait_recv()
        own = own + piece_in[step].astype(F32)
    for copy in rows_out:
        copy.wait_recv()
    own = own + jnp.dot(
        gather_rows,
        gam[...].reshape(n * GROWS, hs),
        precision=lax.Precision.HIGHEST,
        preferred_element_type=F32,
    )
    scen_buf[0] = own
    scen_copies = []
    for step in range(1, n_scen):
        copy = pltpu.make_async_remote_copy(
            src_ref=scen_buf.at[0],
            dst_ref=scen_buf.at[step],
            send_sem=scen_send.at[step],
            recv_sem=scen_recv.at[step],
            device_id={"scen": lax.rem(sc + step, n_scen)},
            device_id_type=MESH,
        )
        copy.start()
        scen_copies.append(copy)
    for h in range(HORIZONS):
        profit_out[:, h, :] = own[0:desk_dev, h * s_dev : (h + 1) * s_dev]

    for copy in scen_copies:
        copy.wait_recv()
    losses = -jnp.transpose(scen_buf[...].reshape(n_scen * GROUP, hs))
    weighted = jnp.zeros((8, 128), F32)
    table = jnp.zeros((8, 128), F32)
    sublane = lax.broadcasted_iota(jnp.int32, (8, 128), 0)
    for h in range(HORIZONS):
        mean = tail_mean(losses[h * s_dev : (h + 1) * s_dev], tail)
        weighted = weighted + horizon_weights[h] * mean * mean
        table = jnp.where(sublane == h, mean, table)
    adjusted = jnp.sqrt(weighted + 1e-06)
    adjusted_out[...] = adjusted[0:1, 0:desk_dev]
    short_out[...] = jnp.transpose(table)[0:desk_dev, 0:HORIZONS]

    for step in steps:
        @pl.when((me + step >= 0) & (me + step < n))
        def _(step=step):
            window_copy(step).wait_send()
    pair.wait_send()
    for copy in pieces + rows_out + scen_copies:
        copy.wait_send()


def local_program(
    n, n_scen,
    loadings, reduced_shocks, sensitivity, cross_gamma, block_list, block_owner, desk_owner, buckets,
):
    f_dev, depth = loadings.shape
    s_dev = reduced_shocks.shape[1]
    desks = sensitivity.shape[1]
    desk_dev = (desks + n - 1) // n + 1
    hs = HORIZONS * s_dev
    nh = n // 2
    tail = (s_dev * n_scen * 25 + 999) // 1000
    smem = pl.BlockSpec(memory_space=pltpu.SMEM)
    vmem = pl.BlockSpec(memory_space=pltpu.VMEM)
    anywhere = pl.BlockSpec(memory_space=pl.ANY)
    dma = pltpu.SemaphoreType.DMA
    profit, shortfall, adjusted = pl.pallas_call(
        functools.partial(kernel, n, n_scen, tail, desk_dev),
        out_shape=(
            jax.ShapeDtypeStruct((desk_dev, HORIZONS, s_dev), F32),
            jax.ShapeDtypeStruct((desk_dev, HORIZONS), F32),
            jax.ShapeDtypeStruct((1, desk_dev), F32),
        ),
        in_specs=[smem, smem, vmem, vmem, anywhere, anywhere, anywhere, anywhere],
        out_specs=(vmem, vmem, vmem),
        scratch_shapes=[
            pltpu.VMEM((f_dev, depth), BF16),
            pltpu.VMEM((depth, s_dev), BF16),
            pltpu.VMEM((f_dev, desks), BF16),
            pltpu.VMEM((CAP, f_dev, f_dev), BF16),
            pltpu.VMEM((WINDOW, s_dev, f_dev), BF16),
            pltpu.VMEM((hs, f_dev), BF16),
            pltpu.VMEM((n * GROUP, hs), F32),
            pltpu.VMEM((nh * GROUP, hs), F32),
            pltpu.VMEM((nh, GROUP, hs), F32),
            pltpu.VMEM((nh, GROUP, hs), BF16),
            pltpu.VMEM((nh, GROUP, hs), BF16),
            pltpu.VMEM((n, GROWS, hs), F32),
            pltpu.VMEM((n_scen, GROUP, hs), F32),
            pltpu.VMEM((1024, 128), F32),
            dma((4,)),
            dma((WINDOW,)),
            dma((WINDOW,)),
            dma((2,)),
            dma((nh,)),
            dma((nh,)),
            dma((n,)),
            dma((n,)),
            dma((n_scen,)),
            dma((n_scen,)),
        ],
        compiler_params=pltpu.CompilerParams(
            collective_id=0, has_side_effects=True, vmem_limit_bytes=40 * 1024 * 1024
        ),
        name="expected_shortfall",
    )(
        block_list,
        block_owner,
        desk_owner.reshape(1, desks),
        buckets.reshape(n, 1, f_dev),
        loadings,
        reduced_shocks,
        sensitivity,
        cross_gamma,
    )
    return profit, shortfall, adjusted.reshape(desk_dev)


def solution(mesh):
    return jax.shard_map(
        functools.partial(local_program, mesh.shape["fac"], mesh.shape["scen"]),
        mesh=mesh,
        in_specs=(
            P("fac", None),
            P(None, "scen"),
            P("fac", None),
            P("fac", None, None),
            P(),
            P(),
            P(),
            P(),
        ),
        out_specs=(P("fac", None, "scen"), P("fac", None), P("fac")),
        check_vma=False,
    )
```

time: 135 us -> 34.6 us (0.26)
  other arithmetic: 41.5 us -> 0 us
  blocking collectives: 34.6 us -> 0 us
  Pallas kernels: 0 us -> 23.6 us
  waiting for transfers between devices: 19.3 us -> 0 us
  starting transfers between devices: 15.8 us -> 0 us
  matrix products: 5.26 us -> 0 us
  loops' own time: 4.32 us -> 0 us
  local copies, waits for them, and re-layouts: 11.9 us -> 9.98 us
    top_k x1 -> x0, other arithmetic: 38.9 us -> none  [local(): worst_losses = lax.top_k(-all_scenarios, tail_count)[0]]
    pallas_call x0 -> x1, Pallas kernels: none -> 23.6 us  [local_program(): pl.pallas_call(functools.partial(kernel, n, n_scen, tail, desk_dev), out_...]
    unnamed x1 -> x0, blocking collectives: 21.5 us -> none
    ppermute x4 -> x0, waiting for transfers between devices: 19 us -> none  [passed_along(): lax.ppermute(value, axis, [(source, source + steps) for source in range(i...]
    all_gather x1 -> x0, blocking collectives: 13.1 us -> none  [local(): all_scenarios = lax.all_gather(profit, 'scen', axis=2, tiled=True)]
    ppermute x4 -> x0, starting transfers between devices: 10.7 us -> none  [passed_along(): lax.ppermute(value, axis, [(source, source + steps) for source in range(i...]
    dot_general x4 -> x0, matrix products: 5.26 us -> none  [the longest x1 2.94 us: add_block(): product = jnp.dot(matrix, col_part, preferred_element_type=jnp.float32)]
    unnamed x2 -> x0, starting transfers between devices: 5.12 us -> none
  transfers between devices with their start and end apart: 6 -> 0, of which waited for: 3 -> 0; matrix products, arithmetic and copies ran while one was open for 4% -> 0% of each run, Pallas kernels for 0% -> 0%
where the time goes in v1:
time: 34.6 us; the launch traced here: 34.3 us
  Pallas kernels  23.6 us (68%)
  local copies, waits for them, and re-layouts  9.98 us (29%)
  between operations  0.71 us (2%)
    pallas_call x1, Pallas kernels, local_program(): pl.pallas_call(functools.partial(kernel, n, n_scen, tail, desk_dev), out_...  23.6 us
    unnamed x15, local copies, waits for them, and re-layouts  9.98 us

profile of v1, /device:TPU:0, one launch (start us, length us, event | category | flops | bytes accessed | tf_op | source)
XLA Modules:
  0.0 34.3 jit_solution(17358896779530739965)
XLA Ops:
  0.6 0.8 %copy.11.blist = s32[12,3]{1,0:T(8,128)S(1)} copy(s32[12,3]{0,1:T(4,128)} %param.12) | data formatting | bytes 288 | tf_op args[4]
  1.4 1.1 %copy.13.reduced = bf16[1000,64]{1,0:T(8,128)(2,1)S(1)} copy(bf16[1000,64]{0,1:T(8,128)(2,1)} %param.9) | data formatting | bytes 256000 | tf_op args[1]
  2.5 1.2 %copy.14.sensitivity = bf16[1024,200]{1,0:T(8,128)(2,1)S(1)} copy(bf16[1024,200]{0,1:T(8,128)(2,1)} %param.10) | data formatting | bytes 819200 | tf_op args[2]
  3.7 0.0 copy-start.1
  3.7 0.0 copy-start.2
  3.7 0.0 copy-start.3
  3.8 2.9 %copy.12.loadings = bf16[1024,1000]{1,0:T(8,128)(2,1)S(1)} copy(bf16[1024,1000]{0,1:T(8,128)(2,1)} %param.8) | data formatting | bytes 4096000 | tf_op args[0]
  6.6 0.0 copy-done.1
  6.6 0.0 copy-done.2
  6.6 0.0 copy-done.3
  6.7 0.0 copy-start
  6.7 2.2 %copy-done = bf16[2,1024,1024]{2,1,0:T(8,128)(2,1)S(1)} copy-done((bf16[2,1024,1024]{2,1,0:T(8,128)(2,1)S(1)}, bf16[2,1024,1024]{2,1,0:T(8,128)(2,1)}, u32[]{:S(2)}) %copy-start) | copy-done | bytes 4194328
  8.8 23.6 %expected_shortfall.1 = (f32[26,5,64]{2,1,0:T(8,128)S(1)}, f32[26,5]{1,0:T(8,128)S(1)}, f32[1,26]{1,0:T(1,128)S(1)}) custom-call(s32[12,3]{1,0:T(8,128)S(1)} %copy.11.blist, s32[12]{0:T(128)S(1)} %copy-done.3, s32[1,200]{1,0:T(1,128)S(1)} %bitcast.4, s32[8,1,1024]{2,1,0:T(1,128)S(1)} %bitcast.3, bf16[1024,1000]{1,0:T(8,128)(2,1)S(1)} %copy.12.loadings, ...), custom_call_target="tpu_custom_call" | custom-call | tf_op jit(solution)/shard_map/expected_shortfall/pallas_call | solution.py:340
  32.5 0.6 %copy.15 = f32[26,5,64]{2,0,1:T(8,128)} copy(f32[26,5,64]{2,1,0:T(8,128)S(1)} %get-tuple-element.9) | data formatting | bytes 66560
  33.1 0.7 %copy.16 = f32[26,5]{0,1:T(8,128)} copy(f32[26,5]{1,0:T(8,128)S(1)} %get-tuple-element.10) | data formatting | bytes 1040
  33.8 0.5 %copy.18 = f32[26]{0:T(128)} copy(f32[26]{0:T(128)S(1)} %bitcast.5) | data formatting | bytes 208
Async XLA Ops:
  3.7 2.9 %copy-start.1 = (s32[8192]{0:T(1024)S(1)}, s32[8192]{0:T(1024)}, u32[]{:S(2)}) copy-start(s32[8192]{0:T(1024)} %param.15) | copy-start | bytes 98308
  3.7 2.9 %copy-start.2 = (s32[200]{0:T(256)S(1)}, s32[200]{0:T(256)}, u32[]{:S(2)}) copy-start(s32[200]{0:T(256)} %param.14) | copy-start | bytes 2404
  3.7 2.9 %copy-start.3 = (s32[12]{0:T(128)S(1)}, s32[12]{0:T(128)}, u32[]{:S(2)}) copy-start(s32[12]{0:T(128)} %bowner.1) | copy-start | bytes 148
  6.7 2.2 %copy-start = (bf16[2,1024,1024]{2,1,0:T(8,128)(2,1)S(1)}, bf16[2,1024,1024]{2,1,0:T(8,128)(2,1)}, u32[]{:S(2)}) copy-start(bf16[2,1024,1024]{2,1,0:T(8,128)(2,1)} %gamma.1) | copy-start | bytes 12582916

commit v2 on v1

v2 whole, which is shorter than its diff:
```python
import functools

import jax
import jax.numpy as jnp
from jax import lax
from jax.experimental import pallas as pl
from jax.experimental.pallas import tpu as pltpu
from jax.sharding import PartitionSpec as P

HORIZONS = 5
CAP = 2
REACH = 2
WINDOW = 2 * REACH + 1
GROUP = 32
PARTS = 2
LANES = 384
LIST = 8
MESH = pl.DeviceIdType.MESH
F32 = jnp.float32
BF16 = jnp.bfloat16

horizon_weights = (1.0, 1.0, 2.0, 2.0, 6.0)


def dot_nt(a, b):
    return lax.dot_general(a, b, (((1,), (1,)), ((), ())), preferred_element_type=F32)


def one_hot(condition):
    return jnp.where(condition, 1.0, 0.0).astype(BF16)


def exchange(items, i, j):
    high, low = jnp.maximum(items[i], items[j]), jnp.minimum(items[i], items[j])
    items[i], items[j] = high, low


SORT8 = (
    (0, 1), (2, 3), (4, 5), (6, 7), (0, 2), (1, 3), (4, 6), (5, 7), (1, 2), (5, 6),
    (0, 4), (1, 5), (2, 6), (3, 7), (2, 4), (3, 5), (1, 2), (3, 4), (5, 6),
)


def merge_sorted(first, second):
    items = [jnp.maximum(first[i], second[LIST - 1 - i]) for i in range(LIST)]
    for stride in (4, 2, 1):
        for i in range(LIST):
            if not i & stride:
                exchange(items, i, i + stride)
    return items


def sorted_tail(losses):
    items = [losses[8 * i : 8 * i + 8] for i in range(LIST)]
    for i, j in SORT8:
        exchange(items, i, j)
    for shift in (4, 2, 1):
        items = merge_sorted(items, [pltpu.roll(item, shift, 0) for item in items])
    return items


def sort_sublanes(tile, sublane, descending):
    for stride in (4, 2, 1):
        first = (sublane & stride) == 0
        other = jnp.where(first, pltpu.roll(tile, 8 - stride, 0), pltpu.roll(tile, stride, 0))
        takes_high = first if descending else jnp.logical_not(first)
        tile = jnp.where(takes_high, jnp.maximum(tile, other), jnp.minimum(tile, other))
    return tile


def tail_kernel(tail, desk_dev, profit, lists, profit_out, short_out, adjusted_out):
    profit_out[...] = profit[:, 0:desk_dev, :]
    shape = (LIST, lists.shape[2])
    sublane = lax.broadcasted_iota(jnp.int32, shape, 0)
    first = sort_sublanes(jnp.maximum(lists[0, 0:8], lists[1, 8:16]), sublane, True)
    second = sort_sublanes(jnp.maximum(lists[2, 0:8], lists[3, 8:16]), sublane, False)
    best = jnp.maximum(first, pltpu.roll(second, LIST - (LIST - tail), 0))
    mean = jnp.sum(jnp.where(sublane < tail, best, 0.0), axis=0, keepdims=True) * (1.0 / tail)
    total = jnp.zeros((1, desk_dev), F32)
    for h in range(HORIZONS):
        row = mean[:, h * GROUP : h * GROUP + desk_dev]
        short_out[h : h + 1, :] = row
        total = total + horizon_weights[h] * row * row
    adjusted_out[...] = jnp.sqrt(total + 1e-06)


def kernel(
    n, n_scen,
    blist, bowner, desk_owner, buckets, loadings, reduced, sensitivity, gamma,
    profit_out, lists_out,
    lbuf, rbuf, sbuf, gbuf, win, masked, terms, pair_buf, totals, piece_out, piece_in,
    gam, lists,
    local_sem, win_send, win_recv, pair_sem, piece_send, piece_recv, gam_send, gam_recv,
    scen_send, scen_recv,
):
    me = lax.axis_index("fac")
    sc = lax.axis_index("scen")
    nh = n // 2
    core, chip = lax.rem(me, 2), me // 2
    s_dev = reduced.shape[0]
    f_dev = loadings.shape[1]
    desks = sensitivity.shape[0]
    blocks = bowner.shape[0]
    hs = HORIZONS * s_dev
    part = f_dev // PARTS

    def columns(i):
        return pl.ds(i * part, part)

    local = [pltpu.make_async_copy(reduced, rbuf, local_sem.at[0])]
    for i in range(PARTS):
        local.append(
            pltpu.make_async_copy(
                loadings.at[:, columns(i)], lbuf.at[:, columns(i)], local_sem.at[1 + i]
            )
        )
    local.append(pltpu.make_async_copy(sensitivity, sbuf, local_sem.at[1 + PARTS]))
    local.append(pltpu.make_async_copy(gamma, gbuf, local_sem.at[2 + PARTS]))
    for copy in local:
        copy.start()

    barrier = pltpu.get_barrier_semaphore()
    for step in range(1, n):
        pl.semaphore_signal(
            barrier, inc=1, device_id={"fac": lax.rem(me + step, n)}, device_id_type=MESH
        )
    for step in range(1, n_scen):
        pl.semaphore_signal(
            barrier, inc=1, device_id={"scen": lax.rem(sc + step, n_scen)}, device_id_type=MESH
        )

    def window_copy(step, i):
        slot = REACH - step
        return pltpu.make_async_remote_copy(
            src_ref=win.at[REACH, :, columns(i)],
            dst_ref=win.at[slot, :, columns(i)],
            send_sem=win_send.at[slot, i],
            recv_sem=win_recv.at[slot, i],
            device_id={"fac": jnp.clip(me + step, 0, n - 1)},
            device_id_type=MESH,
        )

    steps = [step for step in range(-REACH, REACH + 1) if step]
    local[0].wait()
    for i in range(PARTS):
        local[1 + i].wait()
        win[REACH, :, columns(i)] = jnp.dot(
            rbuf[...], lbuf[:, columns(i)], preferred_element_type=F32
        ).astype(BF16)
        if i == 0:
            pl.semaphore_wait(barrier, n - 1 + n_scen - 1)
        for step in steps:
            @pl.when((me + step >= 0) & (me + step < n))
            def _(step=step, i=i):
                window_copy(step, i).start()

    owner_row = desk_owner[...]
    owns = one_hot(lax.broadcasted_iota(jnp.int32, (n, desks), 0) == owner_row)
    before = one_hot(
        lax.broadcasted_iota(jnp.int32, (desks, desks), 0)
        < lax.broadcasted_iota(jnp.int32, (desks, desks), 1)
    )
    earlier = jnp.dot(owns, before, preferred_element_type=F32)
    rank_row = jnp.sum(owns.astype(F32) * earlier, axis=0, keepdims=True).astype(jnp.int32)
    slot_row = ((owner_row & 1) * nh + (owner_row >> 1)) * GROUP + rank_row
    my_group = core * nh + chip

    def fill_masked(shocks, row):
        shocks = shocks.astype(F32)
        for h in range(HORIZONS):
            masked[h * s_dev : (h + 1) * s_dev, :] = jnp.where(row >= h, shocks, 0.0).astype(BF16)

    fill_masked(win[REACH], buckets[me])
    local[1 + PARTS].wait()
    chunk = min(n * GROUP, 256)

    def add_terms(i, carry):
        start = pl.multiple_of(i * chunk, chunk)
        place = one_hot(
            lax.broadcasted_iota(jnp.int32, (chunk, desks), 0) + start == slot_row
        )
        placed = jnp.dot(place, sbuf[...], preferred_element_type=F32).astype(BF16)
        terms[pl.ds(start, chunk), :] = dot_nt(placed, masked[...])
        return carry

    lax.fori_loop(0, n * GROUP // chunk, add_terms, 0)

    half = nh * GROUP
    pair = pltpu.make_async_remote_copy(
        src_ref=terms.at[pl.ds(pl.multiple_of((1 - core) * half, half), half)],
        dst_ref=pair_buf,
        send_sem=pair_sem.at[0],
        recv_sem=pair_sem.at[1],
        device_id={"fac": me + 1 - 2 * core},
        device_id_type=MESH,
    )
    pair.start()

    bpad = (blocks + 15) // 16 * 16
    block_ids = lax.broadcasted_iota(jnp.int32, (bpad, 1), 0)

    def read_block(b, carry):
        count, live, rows, cols, owner_col, desk_col = carry
        owner = bowner[b]
        mine = owner == me
        live = tuple(jnp.where(mine & (count == k), 1, live[k]) for k in range(CAP))
        rows = tuple(jnp.where(mine & (count == k), blist[0, b], rows[k]) for k in range(CAP))
        cols = tuple(jnp.where(mine & (count == k), blist[1, b], cols[k]) for k in range(CAP))
        owner_col = jnp.where(block_ids == b, owner, owner_col)
        desk_col = jnp.where(block_ids == b, blist[2, b], desk_col)
        return count + jnp.where(mine, 1, 0), live, rows, cols, owner_col, desk_col

    empty = jnp.full((bpad, 1), -1, jnp.int32)
    zero = jnp.int32(0)
    _, live, rows, cols, owner_col, desk_col = lax.fori_loop(
        0, blocks, read_block, (zero, (zero,) * CAP, (me,) * CAP, (me,) * CAP, empty, empty)
    )
    block_owns = one_hot(owner_col == lax.broadcasted_iota(jnp.int32, (bpad, n), 1))
    above = one_hot(
        lax.broadcasted_iota(jnp.int32, (bpad, bpad), 0)
        > lax.broadcasted_iota(jnp.int32, (bpad, bpad), 1)
    )
    block_earlier = jnp.dot(above, block_owns, preferred_element_type=F32)
    block_rank = jnp.sum(
        block_owns.astype(F32) * block_earlier, axis=1, keepdims=True
    ).astype(jnp.int32)
    distance = me - owner_col
    distance = jnp.where(distance < 0, distance + n, distance)
    key = jnp.where(owner_col >= 0, block_rank * n + distance, -1)
    key_hot = one_hot(key == lax.broadcasted_iota(jnp.int32, (bpad, CAP * n), 1))
    desk_hot = one_hot(desk_col == lax.broadcasted_iota(jnp.int32, (bpad, desks), 1))
    my_desks = one_hot(
        lax.broadcasted_iota(jnp.int32, (GROUP, desks), 0) + my_group * GROUP == slot_row
    )
    gather_rows = jnp.dot(
        dot_nt(my_desks, desk_hot).astype(BF16), key_hot, preferred_element_type=F32
    )

    pair.wait_recv()
    for j in range(nh):
        start = pl.multiple_of(core * half + j * GROUP, GROUP)
        total = terms[pl.ds(start, GROUP), :] + pair_buf[j * GROUP : (j + 1) * GROUP, :]
        totals[j] = total
        piece_out[j] = total.astype(BF16)
    pieces = []
    for step in range(1, nh):
        target = lax.rem(chip + step, nh)
        copy = pltpu.make_async_remote_copy(
            src_ref=piece_out.at[target],
            dst_ref=piece_in.at[step],
            send_sem=piece_send.at[step],
            recv_sem=piece_recv.at[step],
            device_id={"fac": 2 * target + core},
            device_id_type=MESH,
        )
        copy.start()
        pieces.append(copy)

    for i in range(PARTS):
        for step in steps:
            @pl.when((me - step >= 0) & (me - step < n))
            def _(step=step, i=i):
                window_copy(step, i).wait_recv()
    local[2 + PARTS].wait()
    for k in range(CAP):
        fill_masked(win[jnp.clip(cols[k] - me + REACH, 0, WINDOW - 1)], buckets[cols[k]])
        row_part = win[jnp.clip(rows[k] - me + REACH, 0, WINDOW - 1)].astype(F32)
        row_bucket = buckets[rows[k]]
        folded = [jnp.zeros((s_dev, 128), F32)] * HORIZONS
        for start in range(0, f_dev, 256):
            product = dot_nt(masked[...], gbuf[k, start : start + 256, :])
            for h in range(HORIZONS):
                for i in (0, 128):
                    at = start + i
                    factor = jnp.where(
                        row_bucket[:, at : at + 128] >= h, row_part[:, at : at + 128], 0.0
                    )
                    folded[h] = folded[h] + factor * product[h * s_dev : (h + 1) * s_dev, i : i + 128]
        quad = jnp.sum(jnp.transpose(jnp.concatenate(folded, axis=0)), axis=0, keepdims=True)
        gam[0, :, k * LANES : k * LANES + hs] = quad * (0.5 * live[k].astype(F32))
    rows_out = []
    for step in range(1, n):
        copy = pltpu.make_async_remote_copy(
            src_ref=gam.at[0],
            dst_ref=gam.at[step],
            send_sem=gam_send.at[step],
            recv_sem=gam_recv.at[step],
            device_id={"fac": lax.rem(me + step, n)},
            device_id_type=MESH,
        )
        copy.start()
        rows_out.append(copy)

    own = totals[chip]
    for step, copy in enumerate(pieces, 1):
        copy.wait_recv()
        own = own + piece_in[step].astype(F32)
    for copy in rows_out:
        copy.wait_recv()
    gamma_rows = jnp.concatenate(
        [gam[q, :, k * LANES : k * LANES + hs] for k in range(CAP) for q in range(n)], axis=0
    )
    own = own + jnp.dot(
        gather_rows, gamma_rows, precision=lax.Precision.HIGHEST, preferred_element_type=F32
    )
    stacked = [own[:, h * s_dev : (h + 1) * s_dev] for h in range(HORIZONS)]
    for h in range(HORIZONS):
        profit_out[h] = stacked[h]
    lanes = lists.shape[2]
    stacked.append(jnp.zeros((lanes - HORIZONS * GROUP, s_dev), F32))
    tall = jnp.concatenate(stacked, axis=0)
    tall = jnp.concatenate([tall, jnp.zeros((lanes, 128 - s_dev), F32)], axis=1)
    items = sorted_tail(-jnp.transpose(tall)[0:s_dev])
    sublane = lax.broadcasted_iota(jnp.int32, (LIST, lanes), 0)
    down, up = items[0], items[LIST - 1]
    for i in range(1, LIST):
        down = jnp.where(sublane == i, items[i], down)
        up = jnp.where(sublane == i, items[LIST - 1 - i], up)
    lists[0, 0:LIST] = down
    lists[0, LIST : 2 * LIST] = up
    scen_copies = []
    for step in range(1, n_scen):
        copy = pltpu.make_async_remote_copy(
            src_ref=lists.at[0],
            dst_ref=lists.at[step],
            send_sem=scen_send.at[step],
            recv_sem=scen_recv.at[step],
            device_id={"scen": lax.rem(sc + step, n_scen)},
            device_id_type=MESH,
        )
        copy.start()
        scen_copies.append(copy)

    for i in range(PARTS):
        for step in steps:
            @pl.when((me + step >= 0) & (me + step < n))
            def _(step=step, i=i):
                window_copy(step, i).wait_send()
    pair.wait_send()
    for copy in pieces + rows_out:
        copy.wait_send()
    for copy in scen_copies:
        copy.wait()
    lists_out[...] = lists[...]


def local_program(
    n, n_scen,
    loadings, reduced_shocks, sensitivity, cross_gamma, block_list, block_owner, desk_owner, buckets,
):
    f_dev, depth = loadings.shape
    s_dev = reduced_shocks.shape[1]
    desks = sensitivity.shape[1]
    desk_dev = (desks + n - 1) // n + 1
    hs = HORIZONS * s_dev
    nh = n // 2
    tail = (s_dev * n_scen * 25 + 999) // 1000
    lanes = (HORIZONS * GROUP + 127) // 128 * 128
    smem = pl.BlockSpec(memory_space=pltpu.SMEM)
    vmem = pl.BlockSpec(memory_space=pltpu.VMEM)
    hbm = pl.BlockSpec(memory_space=pltpu.HBM)
    dma = pltpu.SemaphoreType.DMA
    profit, lists = pl.pallas_call(
        functools.partial(kernel, n, n_scen),
        out_shape=(
            jax.ShapeDtypeStruct((HORIZONS, GROUP, s_dev), F32),
            jax.ShapeDtypeStruct((n_scen, 2 * LIST, lanes), F32),
        ),
        in_specs=[smem, smem, vmem, vmem, hbm, hbm, hbm, hbm],
        out_specs=(vmem, vmem),
        scratch_shapes=[
            pltpu.VMEM((depth, f_dev), BF16),
            pltpu.VMEM((s_dev, depth), BF16),
            pltpu.VMEM((desks, f_dev), BF16),
            pltpu.VMEM((CAP, f_dev, f_dev), BF16),
            pltpu.VMEM((WINDOW, s_dev, f_dev), BF16),
            pltpu.VMEM((hs, f_dev), BF16),
            pltpu.VMEM((n * GROUP, hs), F32),
            pltpu.VMEM((nh * GROUP, hs), F32),
            pltpu.VMEM((nh, GROUP, hs), F32),
            pltpu.VMEM((nh, GROUP, hs), BF16),
            pltpu.VMEM((nh, GROUP, hs), BF16),
            pltpu.VMEM((n, 1, CAP * LANES), F32),
            pltpu.VMEM((n_scen, 2 * LIST, lanes), F32),
            dma((3 + PARTS,)),
            dma((WINDOW, PARTS)),
            dma((WINDOW, PARTS)),
            dma((2,)),
            dma((nh,)),
            dma((nh,)),
            dma((n,)),
            dma((n,)),
            dma((n_scen,)),
            dma((n_scen,)),
        ],
        compiler_params=pltpu.CompilerParams(
            collective_id=0, has_side_effects=True, vmem_limit_bytes=55000 * 1024
        ),
        name="profits",
    )(
        block_list.T,
        block_owner,
        desk_owner.reshape(1, desks),
        buckets.reshape(n, 1, f_dev),
        loadings.T,
        reduced_shocks.T,
        sensitivity.T,
        cross_gamma,
    )
    profit, shortfall, adjusted = pl.pallas_call(
        functools.partial(tail_kernel, tail, desk_dev),
        out_shape=(
            jax.ShapeDtypeStruct((HORIZONS, desk_dev, s_dev), F32),
            jax.ShapeDtypeStruct((HORIZONS, desk_dev), F32),
            jax.ShapeDtypeStruct((1, desk_dev), F32),
        ),
        in_specs=[vmem, vmem],
        out_specs=(vmem, vmem, vmem),
        name="tail_means",
    )(profit, lists)
    return jnp.transpose(profit, (1, 0, 2)), shortfall.T, adjusted.reshape(desk_dev)


def solution(mesh):
    return jax.shard_map(
        functools.partial(local_program, mesh.shape["fac"], mesh.shape["scen"]),
        mesh=mesh,
        in_specs=(
            P("fac", None),
            P(None, "scen"),
            P("fac", None),
            P("fac", None, None),
            P(),
            P(),
            P(),
            P(),
        ),
        out_specs=(P("fac", None, "scen"), P("fac", None), P("fac")),
        check_vma=False,
    )
```

time: 34.6 us -> 28 us (0.81)
  local copies, waits for them, and re-layouts: 9.98 us -> 4.02 us
  Pallas kernels: 23.6 us -> 23 us
    unnamed x15 -> x12, local copies, waits for them, and re-layouts: 9.98 us -> 4.02 us
    pallas_call x1 -> x2, Pallas kernels: 23.6 us -> 23 us  [the longest x1 21.4 us: local_program(): pl.pallas_call(functools.partial(kernel, n, n_scen), out_shape=(jax.Shape...]
where the time goes in v2:
time: 28 us; the launch traced here: 27.7 us
  Pallas kernels  23 us (82%)
  local copies, waits for them, and re-layouts  4.02 us (14%)
  between operations  0.66 us (2%)
    pallas_call x1, Pallas kernels, local_program(): pl.pallas_call(functools.partial(kernel, n, n_scen), out_shape=(jax.Shape...  21.4 us
    unnamed x12, local copies, waits for them, and re-layouts  4.02 us
    pallas_call x1, Pallas kernels, local_program(): pl.pallas_call(functools.partial(tail_kernel, tail, desk_dev), out_shape=...  1.58 us

profile of v2, /device:TPU:0, one launch (start us, length us, event | category | flops | bytes accessed | tf_op | source)
XLA Modules:
  0.0 27.7 jit_solution(6976179762310962421)
XLA Ops:
  0.6 0.0 copy-start.2
  0.6 0.7 %copy-done.2 = s32[8192]{0:T(1024)S(1)} copy-done((s32[8192]{0:T(1024)S(1)}, s32[8192]{0:T(1024)}, u32[]{:S(2)}) %copy-start.2) | copy-done | bytes 32792
  1.4 0.0 copy-start.3
  1.4 0.7 %copy-done.3 = s32[12,3]{0,1:T(4,128)S(1)} copy-done((s32[12,3]{0,1:T(4,128)S(1)}, s32[12,3]{0,1:T(4,128)}, u32[]{:S(2)}) %copy-start.3) | copy-done | bytes 168
  2.1 0.0 copy-start.4
  2.1 0.7 %copy-done.4 = s32[200]{0:T(256)S(1)} copy-done((s32[200]{0:T(256)S(1)}, s32[200]{0:T(256)}, u32[]{:S(2)}) %copy-start.4) | copy-done | bytes 824
  2.8 0.0 copy-start.5
  2.8 0.7 %copy-done.5 = s32[12]{0:T(128)S(1)} copy-done((s32[12]{0:T(128)S(1)}, s32[12]{0:T(128)}, u32[]{:S(2)}) %copy-start.5) | copy-done | bytes 72
  3.4 21.4 %profits.1 = (f32[5,32,64]{2,1,0:T(8,128)S(1)}, f32[4,16,256]{2,1,0:T(8,128)S(1)}) custom-call(s32[3,12]{1,0:T(4,128)S(1)} %bitcast.10, s32[12]{0:T(128)S(1)} %copy-done.5, s32[1,200]{1,0:T(1,128)S(1)} %bitcast.11, s32[8,1,1024]{2,1,0:T(1,128)S(1)} %bitcast.9, bf16[1000,1024]{1,0:T(8,128)(2,1)} %bitcast.12, bf16[64,1000]{1,0:T(8,128)(2,1)} %bitcast.14, ...), custom_call_target="tpu_custom_call" | custom-call | tf_op jit(solution)/shard_map/profits/pallas_call | solution.py:363
  24.8 0.0 copy-start
  24.8 0.6 %copy-done = f32[5,32,64]{2,1,0:T(8,128)} copy-done((f32[5,32,64]{2,1,0:T(8,128)}, f32[5,32,64]{2,1,0:T(8,128)S(1)}, u32[]{:S(2)}) %copy-start) | copy-done | bytes 40984
  25.5 0.0 copy-start.1
  25.5 0.6 %copy-done.1 = f32[4,16,256]{2,1,0:T(8,128)} copy-done((f32[4,16,256]{2,1,0:T(8,128)}, f32[4,16,256]{2,1,0:T(8,128)S(1)}, u32[]{:S(2)}) %copy-start.1) | copy-done | bytes 65560
  26.1 1.6 %tail_means.1 = (f32[5,26,64]{2,1,0:T(8,128)}, f32[5,26]{1,0:T(8,128)}, f32[1,26]{1,0:T(1,128)}) custom-call(f32[5,32,64]{2,1,0:T(8,128)} %copy-done, f32[4,16,256]{2,1,0:T(8,128)} %copy-done.1), custom_call_target="tpu_custom_call" | custom-call | tf_op jit(solution)/shard_map/tail_means/pallas_call | solution.py:410
Async XLA Ops:
  0.6 0.8 %copy-start.2 = (s32[8192]{0:T(1024)S(1)}, s32[8192]{0:T(1024)}, u32[]{:S(2)}) copy-start(s32[8192]{0:T(1024)} %param.15) | copy-start | bytes 98308
  1.4 0.7 %copy-start.3 = (s32[12,3]{0,1:T(4,128)S(1)}, s32[12,3]{0,1:T(4,128)}, u32[]{:S(2)}) copy-start(s32[12,3]{0,1:T(4,128)} %param.12) | copy-start | bytes 436
  2.1 0.7 %copy-start.4 = (s32[200]{0:T(256)S(1)}, s32[200]{0:T(256)}, u32[]{:S(2)}) copy-start(s32[200]{0:T(256)} %param.14) | copy-start | bytes 2404
  2.8 0.7 %copy-start.5 = (s32[12]{0:T(128)S(1)}, s32[12]{0:T(128)}, u32[]{:S(2)}) copy-start(s32[12]{0:T(128)} %bowner.1) | copy-start | bytes 148
  24.8 0.6 %copy-start = (f32[5,32,64]{2,1,0:T(8,128)}, f32[5,32,64]{2,1,0:T(8,128)S(1)}, u32[]{:S(2)}) copy-start(f32[5,32,64]{2,1,0:T(8,128)S(1)} %get-tuple-element.8.profit) | copy-start | bytes 122884
  25.5 0.6 %copy-start.1 = (f32[4,16,256]{2,1,0:T(8,128)}, f32[4,16,256]{2,1,0:T(8,128)S(1)}, u32[]{:S(2)}) copy-start(f32[4,16,256]{2,1,0:T(8,128)S(1)} %get-tuple-element.9.lists) | copy-start | bytes 196612

commit v3 on v2

--- a/solution.py
+++ b/solution.py
@@ -14,6 +14,7 @@
 GROUP = 32
 PARTS = 2
 LANES = 384
+GRANT = 63 * 1024 * 1024
 LIST = 8
 MESH = pl.DeviceIdType.MESH
 F32 = jnp.float32
@@ -68,27 +69,25 @@
     return tile
 
 
-def tail_kernel(tail, desk_dev, profit, lists, profit_out, short_out, adjusted_out):
-    profit_out[...] = profit[:, 0:desk_dev, :]
-    shape = (LIST, lists.shape[2])
-    sublane = lax.broadcasted_iota(jnp.int32, shape, 0)
-    first = sort_sublanes(jnp.maximum(lists[0, 0:8], lists[1, 8:16]), sublane, True)
-    second = sort_sublanes(jnp.maximum(lists[2, 0:8], lists[3, 8:16]), sublane, False)
-    best = jnp.maximum(first, pltpu.roll(second, LIST - (LIST - tail), 0))
-    mean = jnp.sum(jnp.where(sublane < tail, best, 0.0), axis=0, keepdims=True) * (1.0 / tail)
-    total = jnp.zeros((1, desk_dev), F32)
-    for h in range(HORIZONS):
-        row = mean[:, h * GROUP : h * GROUP + desk_dev]
-        short_out[h : h + 1, :] = row
-        total = total + horizon_weights[h] * row * row
-    adjusted_out[...] = jnp.sqrt(total + 1e-06)
+def write_kernel(profit, short, adjusted, profit_out, short_out, adjusted_out, sem):
+    copies = [
+        pltpu.make_async_copy(source, target, sem.at[i])
+        for i, (source, target) in enumerate(
+            ((profit, profit_out), (short, short_out), (adjusted, adjusted_out))
+        )
+    ]
+    for copy in copies:
+        copy.start()
+    for copy in copies:
+        copy.wait()
 
 
 def kernel(
-    n, n_scen,
-    blist, bowner, desk_owner, buckets, loadings, reduced, sensitivity, gamma,
-    profit_out, lists_out,
-    lbuf, rbuf, sbuf, gbuf, win, masked, terms, pair_buf, totals, piece_out, piece_in,
+    n, n_scen, tail, desk_dev,
+    blist_in, bowner_in, desk_owner_in, buckets_in, loadings, reduced, sensitivity, gamma,
+    profit_hbm, short_hbm, adjusted_hbm,
+    profit_out, short_out, adjusted_out, out_sem,
+    blist, bowner, desk_owner, buckets, lbuf, rbuf, sbuf, gbuf, win, masked, terms, pair_buf, totals, piece_out, piece_in,
     gam, lists,
     local_sem, win_send, win_recv, pair_sem, piece_send, piece_recv, gam_send, gam_recv,
     scen_send, scen_recv,
@@ -100,7 +99,7 @@
     s_dev = reduced.shape[0]
     f_dev = loadings.shape[1]
     desks = sensitivity.shape[0]
-    blocks = bowner.shape[0]
+    blocks = bowner_in.shape[0]
     hs = HORIZONS * s_dev
     part = f_dev // PARTS
 
@@ -116,7 +115,16 @@
         )
     local.append(pltpu.make_async_copy(sensitivity, sbuf, local_sem.at[1 + PARTS]))
     local.append(pltpu.make_async_copy(gamma, gbuf, local_sem.at[2 + PARTS]))
-    for copy in local:
+    small = [
+        pltpu.make_async_copy(source, target, local_sem.at[3 + PARTS + i])
+        for i, (source, target) in enumerate(
+            (
+                (desk_owner_in, desk_owner), (buckets_in, buckets),
+                (blist_in, blist), (bowner_in, bowner),
+            )
+        )
+    ]
+    for copy in local[: 1 + PARTS] + small + local[1 + PARTS :]:
         copy.start()
 
     barrier = pltpu.get_barrier_semaphore()
@@ -129,30 +137,75 @@
             barrier, inc=1, device_id={"scen": lax.rem(sc + step, n_scen)}, device_id_type=MESH
         )
 
-    def window_copy(step, i):
-        slot = REACH - step
+    partner = me + 1 - 2 * core
+    side = 2 * core - 1
+
+    def window_copy(index, from_slot, to_slot, i, target):
         return pltpu.make_async_remote_copy(
-            src_ref=win.at[REACH, :, columns(i)],
-            dst_ref=win.at[slot, :, columns(i)],
-            send_sem=win_send.at[slot, i],
+            src_ref=win.at[from_slot, i],
+            dst_ref=win.at[to_slot, i],
+            send_sem=win_send.at[index],
+            recv_sem=win_recv.at[to_slot, i],
+            device_id={"fac": jnp.clip(target, 0, n - 1)},
+            device_id_type=MESH,
+        )
+
+    has_both = (chip + side >= 0) & (chip + side < nh)
+    has_one = (chip - side >= 0) & (chip - side < nh)
+    has_left, has_right = chip > 0, chip < nh - 1
+
+    def to_both(i):
+        target = 2 * (chip + side) + i
+        return window_copy(i, REACH, REACH + me - target, i, target)
+
+    def to_one(i):
+        return window_copy(PARTS + i, REACH, REACH + 2 * side, i, me - 2 * side)
+
+    def to_partner(i):
+        return window_copy(2 * PARTS + i, REACH, REACH + me - partner, i, partner)
+
+    left_slot, right_slot = REACH - 1 - core, REACH + 2 - core
+
+    def hand_left():
+        return window_copy(3 * PARTS, left_slot, left_slot + me - partner, core, partner)
+
+    def hand_right():
+        return window_copy(3 * PARTS + 1, right_slot, right_slot + me - partner, core, partner)
+
+    def arrival(slot, i):
+        return pltpu.make_async_remote_copy(
+            src_ref=win.at[REACH, i],
+            dst_ref=win.at[slot, i],
+            send_sem=win_send.at[0],
             recv_sem=win_recv.at[slot, i],
-            device_id={"fac": jnp.clip(me + step, 0, n - 1)},
+            device_id={"fac": partner},
             device_id_type=MESH,
         )
 
-    steps = [step for step in range(-REACH, REACH + 1) if step]
     local[0].wait()
     for i in range(PARTS):
         local[1 + i].wait()
-        win[REACH, :, columns(i)] = jnp.dot(
+        win[REACH, i] = jnp.dot(
             rbuf[...], lbuf[:, columns(i)], preferred_element_type=F32
         ).astype(BF16)
         if i == 0:
             pl.semaphore_wait(barrier, n - 1 + n_scen - 1)
-        for step in steps:
-            @pl.when((me + step >= 0) & (me + step < n))
-            def _(step=step, i=i):
-                window_copy(step, i).start()
+
+        @pl.when(has_both)
+        def _(i=i):
+            to_both(i).start()
+
+        @pl.when(has_one)
+        def _(i=i):
+            to_one(i).start()
+
+        to_partner(i).start()
+
+    def window(slot):
+        return jnp.concatenate([win[slot, i] for i in range(PARTS)], axis=1)
+
+    for copy in small:
+        copy.wait()
 
     owner_row = desk_owner[...]
     owns = one_hot(lax.broadcasted_iota(jnp.int32, (n, desks), 0) == owner_row)
@@ -170,7 +223,7 @@
         for h in range(HORIZONS):
             masked[h * s_dev : (h + 1) * s_dev, :] = jnp.where(row >= h, shocks, 0.0).astype(BF16)
 
-    fill_masked(win[REACH], buckets[me])
+    fill_masked(window(REACH), buckets[me])
     local[1 + PARTS].wait()
     chunk = min(n * GROUP, 256)
 
@@ -191,7 +244,7 @@
         dst_ref=pair_buf,
         send_sem=pair_sem.at[0],
         recv_sem=pair_sem.at[1],
-        device_id={"fac": me + 1 - 2 * core},
+        device_id={"fac": partner},
         device_id_type=MESH,
     )
     pair.start()
@@ -235,6 +288,16 @@
     gather_rows = jnp.dot(
         dot_nt(my_desks, desk_hot).astype(BF16), key_hot, preferred_element_type=F32
     )
+
+    @pl.when(has_left)
+    def _():
+        arrival(left_slot, core).wait_recv()
+        hand_left().start()
+
+    @pl.when(has_right)
+    def _():
+        arrival(right_slot, core).wait_recv()
+        hand_right().start()
 
     pair.wait_recv()
     for j in range(nh):
@@ -257,14 +320,24 @@
         pieces.append(copy)
 
     for i in range(PARTS):
-        for step in steps:
-            @pl.when((me - step >= 0) & (me - step < n))
-            def _(step=step, i=i):
-                window_copy(step, i).wait_recv()
+        arrival(REACH + partner - me, i).wait_recv()
+
+        @pl.when(has_both)
+        def _(i=i):
+            arrival(REACH + 2 * side, i).wait_recv()
+
+    @pl.when(has_left)
+    def _():
+        arrival(left_slot, 1 - core).wait_recv()
+
+    @pl.when(has_right)
+    def _():
+        arrival(right_slot, 1 - core).wait_recv()
+
     local[2 + PARTS].wait()
     for k in range(CAP):
-        fill_masked(win[jnp.clip(cols[k] - me + REACH, 0, WINDOW - 1)], buckets[cols[k]])
-        row_part = win[jnp.clip(rows[k] - me + REACH, 0, WINDOW - 1)].astype(F32)
+        fill_masked(window(jnp.clip(cols[k] - me + REACH, 0, WINDOW - 1)), buckets[cols[k]])
+        row_part = window(jnp.clip(rows[k] - me + REACH, 0, WINDOW - 1)).astype(F32)
         row_bucket = buckets[rows[k]]
         folded = [jnp.zeros((s_dev, 128), F32)] * HORIZONS
         for start in range(0, f_dev, 256):
@@ -305,7 +378,9 @@
     )
     stacked = [own[:, h * s_dev : (h + 1) * s_dev] for h in range(HORIZONS)]
     for h in range(HORIZONS):
-        profit_out[h] = stacked[h]
+        profit_out[h] = stacked[h][0:desk_dev]
+    write_profit = pltpu.make_async_copy(profit_out, profit_hbm, out_sem.at[0])
+    write_profit.start()
     lanes = lists.shape[2]
     stacked.append(jnp.zeros((lanes - HORIZONS * GROUP, s_dev), F32))
     tall = jnp.concatenate(stacked, axis=0)
@@ -332,16 +407,46 @@
         scen_copies.append(copy)
 
     for i in range(PARTS):
-        for step in steps:
-            @pl.when((me + step >= 0) & (me + step < n))
-            def _(step=step, i=i):
-                window_copy(step, i).wait_send()
+        @pl.when(has_both)
+        def _(i=i):
+            to_both(i).wait_send()
+
+        @pl.when(has_one)
+        def _(i=i):
+            to_one(i).wait_send()
+
+        to_partner(i).wait_send()
+
+    @pl.when(has_left)
+    def _():
+        hand_left().wait_send()
+
+    @pl.when(has_right)
+    def _():
+        hand_right().wait_send()
+
     pair.wait_send()
     for copy in pieces + rows_out:
         copy.wait_send()
     for copy in scen_copies:
         copy.wait()
-    lists_out[...] = lists[...]
+
+    first = sort_sublanes(jnp.maximum(lists[0, 0:LIST], lists[1, LIST:]), sublane, True)
+    second = sort_sublanes(jnp.maximum(lists[2, 0:LIST], lists[3, LIST:]), sublane, False)
+    best = jnp.maximum(first, pltpu.roll(second, tail, 0))
+    mean = jnp.sum(jnp.where(sublane < tail, best, 0.0), axis=0, keepdims=True) * (1.0 / tail)
+    total = jnp.zeros((1, desk_dev), F32)
+    for h in range(HORIZONS):
+        row = mean[:, h * GROUP : h * GROUP + desk_dev]
+        short_out[h : h + 1, :] = row
+        total = total + horizon_weights[h] * row * row
+    adjusted_out[...] = jnp.sqrt(total + 1e-06)
+    write_short = pltpu.make_async_copy(short_out, short_hbm, out_sem.at[1])
+    write_adjusted = pltpu.make_async_copy(adjusted_out, adjusted_hbm, out_sem.at[2])
+    write_short.start()
+    write_adjusted.start()
+    for copy in (write_profit, write_short, write_adjusted):
+        copy.wait()
 
 
 def local_program(
@@ -356,24 +461,32 @@
     nh = n // 2
     tail = (s_dev * n_scen * 25 + 999) // 1000
     lanes = (HORIZONS * GROUP + 127) // 128 * 128
-    smem = pl.BlockSpec(memory_space=pltpu.SMEM)
-    vmem = pl.BlockSpec(memory_space=pltpu.VMEM)
-    hbm = pl.BlockSpec(memory_space=pltpu.HBM)
+    anywhere = pl.BlockSpec(memory_space=pl.ANY)
     dma = pltpu.SemaphoreType.DMA
-    profit, lists = pl.pallas_call(
-        functools.partial(kernel, n, n_scen),
-        out_shape=(
-            jax.ShapeDtypeStruct((HORIZONS, GROUP, s_dev), F32),
-            jax.ShapeDtypeStruct((n_scen, 2 * LIST, lanes), F32),
-        ),
-        in_specs=[smem, smem, vmem, vmem, hbm, hbm, hbm, hbm],
-        out_specs=(vmem, vmem),
+    outputs = (
+        jax.ShapeDtypeStruct((HORIZONS, desk_dev, s_dev), F32),
+        jax.ShapeDtypeStruct((HORIZONS, desk_dev), F32),
+        jax.ShapeDtypeStruct((1, desk_dev), F32),
+    )
+    results = pl.pallas_call(
+        functools.partial(kernel, n, n_scen, tail, desk_dev),
+        out_shape=outputs,
+        in_specs=[anywhere] * 8,
+        out_specs=(anywhere,) * 3,
         scratch_shapes=[
+            pltpu.VMEM((HORIZONS, desk_dev, s_dev), F32),
+            pltpu.VMEM((HORIZONS, desk_dev), F32),
+            pltpu.VMEM((1, desk_dev), F32),
+            dma((3,)),
+            pltpu.SMEM((3, block_owner.shape[0]), jnp.int32),
+            pltpu.SMEM((block_owner.shape[0],), jnp.int32),
+            pltpu.VMEM((1, desks), jnp.int32),
+            pltpu.VMEM((n, 1, f_dev), jnp.int32),
             pltpu.VMEM((depth, f_dev), BF16),
             pltpu.VMEM((s_dev, depth), BF16),
             pltpu.VMEM((desks, f_dev), BF16),
             pltpu.VMEM((CAP, f_dev, f_dev), BF16),
-            pltpu.VMEM((WINDOW, s_dev, f_dev), BF16),
+            pltpu.VMEM((WINDOW, PARTS, s_dev, f_dev // PARTS), BF16),
             pltpu.VMEM((hs, f_dev), BF16),
             pltpu.VMEM((n * GROUP, hs), F32),
             pltpu.VMEM((nh * GROUP, hs), F32),
@@ -382,8 +495,8 @@
             pltpu.VMEM((nh, GROUP, hs), BF16),
             pltpu.VMEM((n, 1, CAP * LANES), F32),
             pltpu.VMEM((n_scen, 2 * LIST, lanes), F32),
-            dma((3 + PARTS,)),
-            dma((WINDOW, PARTS)),
+            dma((7 + PARTS,)),
+            dma((3 * PARTS + 2,)),
             dma((WINDOW, PARTS)),
             dma((2,)),
             dma((nh,)),
@@ -394,7 +507,7 @@
             dma((n_scen,)),
         ],
         compiler_params=pltpu.CompilerParams(
-            collective_id=0, has_side_effects=True, vmem_limit_bytes=55000 * 1024
+            collective_id=0, has_side_effects=True, vmem_limit_bytes=GRANT
         ),
         name="profits",
     )(
@@ -408,16 +521,14 @@
         cross_gamma,
     )
     profit, shortfall, adjusted = pl.pallas_call(
-        functools.partial(tail_kernel, tail, desk_dev),
-        out_shape=(
-            jax.ShapeDtypeStruct((HORIZONS, desk_dev, s_dev), F32),
-            jax.ShapeDtypeStruct((HORIZONS, desk_dev), F32),
-            jax.ShapeDtypeStruct((1, desk_dev), F32),
-        ),
-        in_specs=[vmem, vmem],
-        out_specs=(vmem, vmem, vmem),
-        name="tail_means",
-    )(profit, lists)
+        write_kernel,
+        out_shape=outputs,
+        in_specs=[anywhere] * 3,
+        out_specs=(anywhere,) * 3,
+        scratch_shapes=[dma((3,))],
+        compiler_params=pltpu.CompilerParams(vmem_limit_bytes=GRANT),
+        name="write_results",
+    )(*results)
     return jnp.transpose(profit, (1, 0, 2)), shortfall.T, adjusted.reshape(desk_dev)
 
 

time: 28 us -> 24.6 us (0.88)
  local copies, waits for them, and re-layouts: 4.02 us -> 0 us
  Pallas kernels: 23 us -> 23.9 us
    unnamed x12 -> x0, local copies, waits for them, and re-layouts: 4.02 us -> none
    pallas_call x2, Pallas kernels: 23 us -> 23.9 us  [the longest x1 20.6 us: local_program(): pl.pallas_call(functools.partial(kernel, n, n_scen, tail, desk_dev), out_...]
where the time goes in v3:
time: 24.6 us; the launch traced here: 24.5 us
  Pallas kernels  23.9 us (97%)
  between operations  0.64 us (3%)
    pallas_call x1, Pallas kernels, local_program(): pl.pallas_call(functools.partial(kernel, n, n_scen, tail, desk_dev), out_...  20.6 us
    pallas_call x1, Pallas kernels, local_program(): pl.pallas_call(write_kernel, out_shape=outputs, in_specs=[anywhere] * 3,...  3.24 us

profile of v3, /device:TPU:0, one launch (start us, length us, event | category | flops | bytes accessed | tf_op | source)
XLA Modules:
  0.0 24.5 jit_solution(13680166732887193948)
XLA Ops:
  0.6 20.6 %profits.1 = (f32[5,26,64]{2,1,0:T(8,128)}, f32[5,26]{1,0:T(8,128)}, f32[1,26]{1,0:T(1,128)}) custom-call(s32[3,12]{1,0:T(4,128)} %bitcast.13, s32[12]{0:T(128)} %bowner_in.1, s32[1,200]{1,0:T(1,128)} %bitcast.14, s32[8,1,1024]{2,1,0:T(1,128)} %bitcast.12, bf16[1000,1024]{1,0:T(8,128)(2,1)} %bitcast.9, bf16[64,1000]{1,0:T(8,128)(2,1)} %bitcast.11, ...), custom_call_target="tpu_custom_call" | custom-call | tf_op jit(solution)/shard_map/profits/pallas_call | solution.py:471
  21.3 3.2 %write_results.1 = (f32[5,26,64]{2,1,0:T(8,128)}, f32[5,26]{1,0:T(8,128)}, f32[1,26]{1,0:T(1,128)}) custom-call(f32[5,26,64]{2,1,0:T(8,128)} %get-tuple-element.9.profit, f32[5,26]{1,0:T(8,128)} %get-tuple-element.10.short, f32[1,26]{1,0:T(1,128)} %get-tuple-element.11.adjusted), custom_call_target="tpu_custom_call" | custom-call | tf_op jit(solution)/shard_map/write_results/pallas_call | solution.py:523

commit v4 on v3

--- a/solution.py
+++ b/solution.py
@@ -69,16 +69,24 @@
     return tile
 
 
-def write_kernel(profit, short, adjusted, profit_out, short_out, adjusted_out, sem):
-    copies = [
-        pltpu.make_async_copy(source, target, sem.at[i])
-        for i, (source, target) in enumerate(
-            ((profit, profit_out), (short, short_out), (adjusted, adjusted_out))
-        )
+def write_kernel(
+    profit, short, adjusted, profit_out, short_out, adjusted_out, profit_v, short_v, adjusted_v, sem
+):
+    held = (profit_v, short_v, adjusted_v)
+    first = [
+        pltpu.make_async_copy(source, target, sem.at[0, i])
+        for i, (source, target) in enumerate(zip((profit, short, adjusted), held))
     ]
-    for copy in copies:
+    second = [
+        pltpu.make_async_copy(source, target, sem.at[1, i])
+        for i, (source, target) in enumerate(zip(held, (profit_out, short_out, adjusted_out)))
+    ]
+    for copy in first:
         copy.start()
-    for copy in copies:
+    for before, copy in zip(first, second):
+        before.wait()
+        copy.start()
+    for copy in second:
         copy.wait()
 
 
@@ -289,16 +297,6 @@
         dot_nt(my_desks, desk_hot).astype(BF16), key_hot, preferred_element_type=F32
     )
 
-    @pl.when(has_left)
-    def _():
-        arrival(left_slot, core).wait_recv()
-        hand_left().start()
-
-    @pl.when(has_right)
-    def _():
-        arrival(right_slot, core).wait_recv()
-        hand_right().start()
-
     pair.wait_recv()
     for j in range(nh):
         start = pl.multiple_of(core * half + j * GROUP, GROUP)
@@ -318,6 +316,16 @@
         )
         copy.start()
         pieces.append(copy)
+
+    @pl.when(has_left)
+    def _():
+        arrival(left_slot, core).wait_recv()
+        hand_left().start()
+
+    @pl.when(has_right)
+    def _():
+        arrival(right_slot, core).wait_recv()
+        hand_right().start()
 
     for i in range(PARTS):
         arrival(REACH + partner - me, i).wait_recv()
@@ -525,7 +533,7 @@
         out_shape=outputs,
         in_specs=[anywhere] * 3,
         out_specs=(anywhere,) * 3,
-        scratch_shapes=[dma((3,))],
+        scratch_shapes=[pltpu.VMEM(out.shape, F32) for out in outputs] + [dma((2, 3))],
         compiler_params=pltpu.CompilerParams(vmem_limit_bytes=GRANT),
         name="write_results",
     )(*results)

time: 24.6 us -> 23 us (0.935)
  Pallas kernels: 23.9 us -> 22.2 us
    pallas_call x1, Pallas kernels: 3.24 us -> 1.57 us  [local_program(): pl.pallas_call(write_kernel, out_shape=outputs, in_specs=[anywhere] * 3,...]
where the time goes in v4:
time: 23 us; the launch traced here: 22.8 us
  Pallas kernels  22.2 us (97%)
  between operations  0.64 us (3%)
    pallas_call x1, Pallas kernels, local_program(): pl.pallas_call(functools.partial(kernel, n, n_scen, tail, desk_dev), out_...  20.6 us
    pallas_call x1, Pallas kernels, local_program(): pl.pallas_call(write_kernel, out_shape=outputs, in_specs=[anywhere] * 3,...  1.57 us

profile of v4, /device:TPU:0, one launch (start us, length us, event | category | flops | bytes accessed | tf_op | source)
XLA Modules:
  0.0 22.8 jit_solution(14237399526664646684)
XLA Ops:
  0.6 20.6 %profits.1 = (f32[5,26,64]{2,1,0:T(8,128)}, f32[5,26]{1,0:T(8,128)}, f32[1,26]{1,0:T(1,128)}) custom-call(s32[3,12]{1,0:T(4,128)} %bitcast.13, s32[12]{0:T(128)} %bowner_in.1, s32[1,200]{1,0:T(1,128)} %bitcast.14, s32[8,1,1024]{2,1,0:T(1,128)} %bitcast.12, bf16[1000,1024]{1,0:T(8,128)(2,1)} %bitcast.9, bf16[64,1000]{1,0:T(8,128)(2,1)} %bitcast.11, ...), custom_call_target="tpu_custom_call" | custom-call | tf_op jit(solution)/shard_map/profits/pallas_call | solution.py:479
  21.3 1.6 %write_results.1 = (f32[5,26,64]{2,1,0:T(8,128)}, f32[5,26]{1,0:T(8,128)}, f32[1,26]{1,0:T(1,128)}) custom-call(f32[5,26,64]{2,1,0:T(8,128)} %get-tuple-element.9.profit, f32[5,26]{1,0:T(8,128)} %get-tuple-element.10.short, f32[1,26]{1,0:T(1,128)} %get-tuple-element.11.adjusted), custom_call_target="tpu_custom_call" | custom-call | tf_op jit(solution)/shard_map/write_results/pallas_call | solution.py:531

commit v5 on v4

--- a/solution.py
+++ b/solution.py
@@ -70,31 +70,43 @@
 
 
 def write_kernel(
-    profit, short, adjusted, profit_out, short_out, adjusted_out, profit_v, short_v, adjusted_v, sem
+    tail, desk_dev,
+    profit, lists_in, profit_out, short_out, adjusted_out, profit_v, lists, short_v, adjusted_v, sem,
 ):
-    held = (profit_v, short_v, adjusted_v)
-    first = [
-        pltpu.make_async_copy(source, target, sem.at[0, i])
-        for i, (source, target) in enumerate(zip((profit, short, adjusted), held))
+    read_lists = pltpu.make_async_copy(lists_in, lists, sem.at[0])
+    read_profit = pltpu.make_async_copy(profit, profit_v, sem.at[1])
+    read_lists.start()
+    read_profit.start()
+    read_profit.wait()
+    writes = [
+        pltpu.make_async_copy(source, target, sem.at[2 + i])
+        for i, (source, target) in enumerate(
+            ((profit_v, profit_out), (short_v, short_out), (adjusted_v, adjusted_out))
+        )
     ]
-    second = [
-        pltpu.make_async_copy(source, target, sem.at[1, i])
-        for i, (source, target) in enumerate(zip(held, (profit_out, short_out, adjusted_out)))
-    ]
-    for copy in first:
+    writes[0].start()
+    read_lists.wait()
+    sublane = lax.broadcasted_iota(jnp.int32, (LIST, lists.shape[2]), 0)
+    first = sort_sublanes(jnp.maximum(lists[0, 0:LIST], lists[1, LIST:]), sublane, True)
+    second = sort_sublanes(jnp.maximum(lists[2, 0:LIST], lists[3, LIST:]), sublane, False)
+    best = jnp.maximum(first, pltpu.roll(second, tail, 0))
+    mean = jnp.sum(jnp.where(sublane < tail, best, 0.0), axis=0, keepdims=True) * (1.0 / tail)
+    total = jnp.zeros((1, desk_dev), F32)
+    for h in range(HORIZONS):
+        row = mean[:, h * GROUP : h * GROUP + desk_dev]
+        short_v[h : h + 1, :] = row
+        total = total + horizon_weights[h] * row * row
+    adjusted_v[...] = jnp.sqrt(total + 1e-06)
+    for copy in writes[1:]:
         copy.start()
-    for before, copy in zip(first, second):
-        before.wait()
-        copy.start()
-    for copy in second:
+    for copy in writes:
         copy.wait()
 
 
 def kernel(
-    n, n_scen, tail, desk_dev,
+    n, n_scen, desk_dev,
     blist_in, bowner_in, desk_owner_in, buckets_in, loadings, reduced, sensitivity, gamma,
-    profit_hbm, short_hbm, adjusted_hbm,
-    profit_out, short_out, adjusted_out, out_sem,
+    profit_hbm, lists_hbm, profit_out, out_sem,
     blist, bowner, desk_owner, buckets, lbuf, rbuf, sbuf, gbuf, win, masked, terms, pair_buf, totals, piece_out, piece_in,
     gam, lists,
     local_sem, win_send, win_recv, pair_sem, piece_send, piece_recv, gam_send, gam_recv,
@@ -226,12 +238,11 @@
     slot_row = ((owner_row & 1) * nh + (owner_row >> 1)) * GROUP + rank_row
     my_group = core * nh + chip
 
-    def fill_masked(shocks, row):
-        shocks = shocks.astype(F32)
+    def fill_masked(k, shocks, row):
         for h in range(HORIZONS):
-            masked[h * s_dev : (h + 1) * s_dev, :] = jnp.where(row >= h, shocks, 0.0).astype(BF16)
-
-    fill_masked(window(REACH), buckets[me])
+            masked[k, h * s_dev : (h + 1) * s_dev, :] = shocks * one_hot(row >= h)
+
+    fill_masked(CAP, window(REACH), buckets[me])
     local[1 + PARTS].wait()
     chunk = min(n * GROUP, 256)
 
@@ -241,7 +252,7 @@
             lax.broadcasted_iota(jnp.int32, (chunk, desks), 0) + start == slot_row
         )
         placed = jnp.dot(place, sbuf[...], preferred_element_type=F32).astype(BF16)
-        terms[pl.ds(start, chunk), :] = dot_nt(placed, masked[...])
+        terms[pl.ds(start, chunk), :] = dot_nt(placed, masked[CAP])
         return carry
 
     lax.fori_loop(0, n * GROUP // chunk, add_terms, 0)
@@ -344,12 +355,13 @@
 
     local[2 + PARTS].wait()
     for k in range(CAP):
-        fill_masked(window(jnp.clip(cols[k] - me + REACH, 0, WINDOW - 1)), buckets[cols[k]])
+        fill_masked(k, window(jnp.clip(cols[k] - me + REACH, 0, WINDOW - 1)), buckets[cols[k]])
+    for k in range(CAP):
         row_part = window(jnp.clip(rows[k] - me + REACH, 0, WINDOW - 1)).astype(F32)
         row_bucket = buckets[rows[k]]
         folded = [jnp.zeros((s_dev, 128), F32)] * HORIZONS
         for start in range(0, f_dev, 256):
-            product = dot_nt(masked[...], gbuf[k, start : start + 256, :])
+            product = dot_nt(masked[k], gbuf[k, start : start + 256, :])
             for h in range(HORIZONS):
                 for i in (0, 128):
                     at = start + i
@@ -389,7 +401,7 @@
         profit_out[h] = stacked[h][0:desk_dev]
     write_profit = pltpu.make_async_copy(profit_out, profit_hbm, out_sem.at[0])
     write_profit.start()
-    lanes = lists.shape[2]
+    lanes = lists.shape[1]
     stacked.append(jnp.zeros((lanes - HORIZONS * GROUP, s_dev), F32))
     tall = jnp.concatenate(stacked, axis=0)
     tall = jnp.concatenate([tall, jnp.zeros((lanes, 128 - s_dev), F32)], axis=1)
@@ -399,13 +411,13 @@
     for i in range(1, LIST):
         down = jnp.where(sublane == i, items[i], down)
         up = jnp.where(sublane == i, items[LIST - 1 - i], up)
-    lists[0, 0:LIST] = down
-    lists[0, LIST : 2 * LIST] = up
+    lists[0:LIST] = down
+    lists[LIST : 2 * LIST] = up
     scen_copies = []
     for step in range(1, n_scen):
         copy = pltpu.make_async_remote_copy(
-            src_ref=lists.at[0],
-            dst_ref=lists.at[step],
+            src_ref=lists,
+            dst_ref=lists_hbm.at[step],
             send_sem=scen_send.at[step],
             recv_sem=scen_recv.at[step],
             device_id={"scen": lax.rem(sc + step, n_scen)},
@@ -413,6 +425,8 @@
         )
         copy.start()
         scen_copies.append(copy)
+    write_lists = pltpu.make_async_copy(lists, lists_hbm.at[0], out_sem.at[1])
+    write_lists.start()
 
     for i in range(PARTS):
         @pl.when(has_both)
@@ -439,22 +453,8 @@
     for copy in scen_copies:
         copy.wait()
 
-    first = sort_sublanes(jnp.maximum(lists[0, 0:LIST], lists[1, LIST:]), sublane, True)
-    second = sort_sublanes(jnp.maximum(lists[2, 0:LIST], lists[3, LIST:]), sublane, False)
-    best = jnp.maximum(first, pltpu.roll(second, tail, 0))
-    mean = jnp.sum(jnp.where(sublane < tail, best, 0.0), axis=0, keepdims=True) * (1.0 / tail)
-    total = jnp.zeros((1, desk_dev), F32)
-    for h in range(HORIZONS):
-        row = mean[:, h * GROUP : h * GROUP + desk_dev]
-        short_out[h : h + 1, :] = row
-        total = total + horizon_weights[h] * row * row
-    adjusted_out[...] = jnp.sqrt(total + 1e-06)
-    write_short = pltpu.make_async_copy(short_out, short_hbm, out_sem.at[1])
-    write_adjusted = pltpu.make_async_copy(adjusted_out, adjusted_hbm, out_sem.at[2])
-    write_short.start()
-    write_adjusted.start()
-    for copy in (write_profit, write_short, write_adjusted):
-        copy.wait()
+    write_profit.wait()
+    write_lists.wait()
 
 
 def local_program(
@@ -477,15 +477,13 @@
         jax.ShapeDtypeStruct((1, desk_dev), F32),
     )
     results = pl.pallas_call(
-        functools.partial(kernel, n, n_scen, tail, desk_dev),
-        out_shape=outputs,
+        functools.partial(kernel, n, n_scen, desk_dev),
+        out_shape=(outputs[0], jax.ShapeDtypeStruct((n_scen, 2 * LIST, lanes), F32)),
         in_specs=[anywhere] * 8,
-        out_specs=(anywhere,) * 3,
+        out_specs=(anywhere,) * 2,
         scratch_shapes=[
             pltpu.VMEM((HORIZONS, desk_dev, s_dev), F32),
-            pltpu.VMEM((HORIZONS, desk_dev), F32),
-            pltpu.VMEM((1, desk_dev), F32),
-            dma((3,)),
+            dma((2,)),
             pltpu.SMEM((3, block_owner.shape[0]), jnp.int32),
             pltpu.SMEM((block_owner.shape[0],), jnp.int32),
             pltpu.VMEM((1, desks), jnp.int32),
@@ -495,14 +493,14 @@
             pltpu.VMEM((desks, f_dev), BF16),
             pltpu.VMEM((CAP, f_dev, f_dev), BF16),
             pltpu.VMEM((WINDOW, PARTS, s_dev, f_dev // PARTS), BF16),
-            pltpu.VMEM((hs, f_dev), BF16),
+            pltpu.VMEM((CAP + 1, hs, f_dev), BF16),
             pltpu.VMEM((n * GROUP, hs), F32),
             pltpu.VMEM((nh * GROUP, hs), F32),
             pltpu.VMEM((nh, GROUP, hs), F32),
             pltpu.VMEM((nh, GROUP, hs), BF16),
             pltpu.VMEM((nh, GROUP, hs), BF16),
             pltpu.VMEM((n, 1, CAP * LANES), F32),
-            pltpu.VMEM((n_scen, 2 * LIST, lanes), F32),
+            pltpu.VMEM((2 * LIST, lanes), F32),
             dma((7 + PARTS,)),
             dma((3 * PARTS + 2,)),
             dma((WINDOW, PARTS)),
@@ -529,11 +527,17 @@
         cross_gamma,
     )
     profit, shortfall, adjusted = pl.pallas_call(
-        write_kernel,
+        functools.partial(write_kernel, tail, desk_dev),
         out_shape=outputs,
-        in_specs=[anywhere] * 3,
+        in_specs=[anywhere] * 2,
         out_specs=(anywhere,) * 3,
-        scratch_shapes=[pltpu.VMEM(out.shape, F32) for out in outputs] + [dma((2, 3))],
+        scratch_shapes=[
+            pltpu.VMEM(outputs[0].shape, F32),
+            pltpu.VMEM((n_scen, 2 * LIST, lanes), F32),
+            pltpu.VMEM(outputs[1].shape, F32),
+            pltpu.VMEM(outputs[2].shape, F32),
+            dma((5,)),
+        ],
         compiler_params=pltpu.CompilerParams(vmem_limit_bytes=GRANT),
         name="write_results",
     )(*results)

time: 23 us -> 22.5 us (0.978)
  Pallas kernels: 22.2 us -> 21.7 us
    pallas_call x2, Pallas kernels: 22.2 us -> 21.7 us  [the longest x1 20 us: local_program(): pl.pallas_call(functools.partial(kernel, n, n_scen, desk_dev), out_shape=...]
where the time goes in v5:
time: 22.5 us; the launch traced here: 22.3 us
  Pallas kernels  21.7 us (96%)
  between operations  0.64 us (3%)
    pallas_call x1, Pallas kernels, local_program(): pl.pallas_call(functools.partial(kernel, n, n_scen, desk_dev), out_shape=...  20 us
    pallas_call x1, Pallas kernels, local_program(): pl.pallas_call(functools.partial(write_kernel, tail, desk_dev), out_shape...  1.64 us

profile of v5, /device:TPU:0, one launch (start us, length us, event | category | flops | bytes accessed | tf_op | source)
XLA Modules:
  0.0 22.3 jit_solution(14093181434657060740)
XLA Ops:
  0.6 20.0 %profits.1 = (f32[5,26,64]{2,1,0:T(8,128)}, f32[4,16,256]{2,1,0:T(8,128)}) custom-call(s32[3,12]{1,0:T(4,128)} %bitcast.13, s32[12]{0:T(128)} %bowner_in.1, s32[1,200]{1,0:T(1,128)} %bitcast.14, s32[8,1,1024]{2,1,0:T(1,128)} %bitcast.12, bf16[1000,1024]{1,0:T(8,128)(2,1)} %bitcast.9, bf16[64,1000]{1,0:T(8,128)(2,1)} %bitcast.11, bf16[200,1024]{1,0:T(8,128)(2,1)} %bitcast.10, ...), custom_call_target="tpu_custom_call" | custom-call | tf_op jit(solution)/shard_map/profits/pallas_call | solution.py:479
  20.7 1.6 %write_results.1 = (f32[5,26,64]{2,1,0:T(8,128)}, f32[5,26]{1,0:T(8,128)}, f32[1,26]{1,0:T(1,128)}) custom-call(f32[5,26,64]{2,1,0:T(8,128)} %get-tuple-element.8.profit, f32[4,16,256]{2,1,0:T(8,128)} %get-tuple-element.9.lists_in), custom_call_target="tpu_custom_call" | custom-call | tf_op jit(solution)/shard_map/write_results/pallas_call | solution.py:529

commit v6 on v5

--- a/solution.py
+++ b/solution.py
@@ -215,10 +215,6 @@
         def _(i=i):
             to_both(i).start()
 
-        @pl.when(has_one)
-        def _(i=i):
-            to_one(i).start()
-
         to_partner(i).start()
 
     def window(slot):
@@ -267,6 +263,11 @@
         device_id_type=MESH,
     )
     pair.start()
+
+    @pl.when(has_one)
+    def _():
+        for i in range(PARTS):
+            to_one(i).start()
 
     bpad = (blocks + 15) // 16 * 16
     block_ids = lax.broadcasted_iota(jnp.int32, (bpad, 1), 0)

time: 22.5 us -> 23.1 us (1.027)
  Pallas kernels: 21.7 us -> 22.3 us
    pallas_call x1, Pallas kernels: 20 us -> 20.6 us  [local_program(): pl.pallas_call(functools.partial(kernel, n, n_scen, desk_dev), out_shape=...]
where the time goes in v6:
time: 23.1 us; the launch traced here: 22.9 us
  Pallas kernels  22.3 us (97%)
  between operations  0.64 us (3%)
    pallas_call x1, Pallas kernels, local_program(): pl.pallas_call(functools.partial(kernel, n, n_scen, desk_dev), out_shape=...  20.6 us
    pallas_call x1, Pallas kernels, local_program(): pl.pallas_call(functools.partial(write_kernel, tail, desk_dev), out_shape...  1.64 us

profile of v6, /device:TPU:0, one launch (start us, length us, event | category | flops | bytes accessed | tf_op | source)
XLA Modules:
  0.0 22.9 jit_solution(994419895699999991)
XLA Ops:
  0.6 20.6 %profits.1 = (f32[5,26,64]{2,1,0:T(8,128)}, f32[4,16,256]{2,1,0:T(8,128)}) custom-call(s32[3,12]{1,0:T(4,128)} %bitcast.13, s32[12]{0:T(128)} %bowner_in.1, s32[1,200]{1,0:T(1,128)} %bitcast.14, s32[8,1,1024]{2,1,0:T(1,128)} %bitcast.12, bf16[1000,1024]{1,0:T(8,128)(2,1)} %bitcast.9, bf16[64,1000]{1,0:T(8,128)(2,1)} %bitcast.11, bf16[200,1024]{1,0:T(8,128)(2,1)} %bitcast.10, ...), custom_call_target="tpu_custom_call" | custom-call | tf_op jit(solution)/shard_map/profits/pallas_call | solution.py:480
  21.3 1.6 %write_results.1 = (f32[5,26,64]{2,1,0:T(8,128)}, f32[5,26]{1,0:T(8,128)}, f32[1,26]{1,0:T(1,128)}) custom-call(f32[5,26,64]{2,1,0:T(8,128)} %get-tuple-element.8.profit, f32[4,16,256]{2,1,0:T(8,128)} %get-tuple-element.9.lists_in), custom_call_target="tpu_custom_call" | custom-call | tf_op jit(solution)/shard_map/write_results/pallas_call | solution.py:530

commit v7 on v6

--- a/solution.py
+++ b/solution.py
@@ -13,6 +13,7 @@
 WINDOW = 2 * REACH + 1
 GROUP = 32
 PARTS = 2
+PIECES = 2
 LANES = 384
 GRANT = 63 * 1024 * 1024
 LIST = 8
@@ -109,7 +110,7 @@
     profit_hbm, lists_hbm, profit_out, out_sem,
     blist, bowner, desk_owner, buckets, lbuf, rbuf, sbuf, gbuf, win, masked, terms, pair_buf, totals, piece_out, piece_in,
     gam, lists,
-    local_sem, win_send, win_recv, pair_sem, piece_send, piece_recv, gam_send, gam_recv,
+    local_sem, load_sem, win_send, win_recv, pair_sem, piece_send, piece_recv, gam_send, gam_recv,
     scen_send, scen_recv,
 ):
     me = lax.axis_index("fac")
@@ -126,17 +127,29 @@
     def columns(i):
         return pl.ds(i * part, part)
 
-    local = [pltpu.make_async_copy(reduced, rbuf, local_sem.at[0])]
-    for i in range(PARTS):
-        local.append(
-            pltpu.make_async_copy(
-                loadings.at[:, columns(i)], lbuf.at[:, columns(i)], local_sem.at[1 + i]
-            )
-        )
-    local.append(pltpu.make_async_copy(sensitivity, sbuf, local_sem.at[1 + PARTS]))
-    local.append(pltpu.make_async_copy(gamma, gbuf, local_sem.at[2 + PARTS]))
+    load_reduced = pltpu.make_async_copy(reduced, rbuf, local_sem.at[0])
+    load_sensitivity = pltpu.make_async_copy(sensitivity, sbuf, local_sem.at[1])
+    piece = part // PIECES
+    load_loadings = [
+        pltpu.make_async_copy(
+            loadings.at[:, pl.ds(i * piece, piece)],
+            lbuf.at[:, pl.ds(i * piece, piece)],
+            load_sem.at[0, i],
+        )
+        for i in range(PARTS * PIECES)
+    ]
+    rows_each = f_dev // PIECES
+    load_gamma = [
+        pltpu.make_async_copy(
+            gamma.at[k, pl.ds(i * rows_each, rows_each)],
+            gbuf.at[k, pl.ds(i * rows_each, rows_each)],
+            load_sem.at[1, k * PIECES + i],
+        )
+        for k in range(CAP)
+        for i in range(PIECES)
+    ]
     small = [
-        pltpu.make_async_copy(source, target, local_sem.at[3 + PARTS + i])
+        pltpu.make_async_copy(source, target, local_sem.at[2 + i])
         for i, (source, target) in enumerate(
             (
                 (desk_owner_in, desk_owner), (buckets_in, buckets),
@@ -144,7 +157,7 @@
             )
         )
     ]
-    for copy in local[: 1 + PARTS] + small + local[1 + PARTS :]:
+    for copy in [load_reduced] + load_loadings + small:
         copy.start()
 
     barrier = pltpu.get_barrier_semaphore()
@@ -202,9 +215,13 @@
             device_id_type=MESH,
         )
 
-    local[0].wait()
+    load_reduced.wait()
     for i in range(PARTS):
-        local[1 + i].wait()
+        for copy in load_loadings[i * PIECES : (i + 1) * PIECES]:
+            copy.wait()
+        if i == PARTS - 1:
+            for copy in [load_sensitivity] + load_gamma:
+                copy.start()
         win[REACH, i] = jnp.dot(
             rbuf[...], lbuf[:, columns(i)], preferred_element_type=F32
         ).astype(BF16)
@@ -239,7 +256,7 @@
             masked[k, h * s_dev : (h + 1) * s_dev, :] = shocks * one_hot(row >= h)
 
     fill_masked(CAP, window(REACH), buckets[me])
-    local[1 + PARTS].wait()
+    load_sensitivity.wait()
     chunk = min(n * GROUP, 256)
 
     def add_terms(i, carry):
@@ -354,7 +371,8 @@
     def _():
         arrival(right_slot, 1 - core).wait_recv()
 
-    local[2 + PARTS].wait()
+    for copy in load_gamma:
+        copy.wait()
     for k in range(CAP):
         fill_masked(k, window(jnp.clip(cols[k] - me + REACH, 0, WINDOW - 1)), buckets[cols[k]])
     for k in range(CAP):
@@ -502,7 +520,8 @@
             pltpu.VMEM((nh, GROUP, hs), BF16),
             pltpu.VMEM((n, 1, CAP * LANES), F32),
             pltpu.VMEM((2 * LIST, lanes), F32),
-            dma((7 + PARTS,)),
+            dma((6,)),
+            dma((2, max(PARTS, CAP) * PIECES)),
             dma((3 * PARTS + 2,)),
             dma((WINDOW, PARTS)),
             dma((2,)),

time: 23.1 us -> 24.6 us (1.065)
  Pallas kernels: 22.3 us -> 23.7 us
    pallas_call x1, Pallas kernels: 20.6 us -> 22.1 us  [local_program(): pl.pallas_call(functools.partial(kernel, n, n_scen, desk_dev), out_shape=...]
where the time goes in v7:
time: 24.6 us; the launch traced here: 24.4 us
  Pallas kernels  23.7 us (96%)
  between operations  0.64 us (3%)
    pallas_call x1, Pallas kernels, local_program(): pl.pallas_call(functools.partial(kernel, n, n_scen, desk_dev), out_shape=...  22.1 us
    pallas_call x1, Pallas kernels, local_program(): pl.pallas_call(functools.partial(write_kernel, tail, desk_dev), out_shape...  1.64 us

profile of v7, /device:TPU:0, one launch (start us, length us, event | category | flops | bytes accessed | tf_op | source)
XLA Modules:
  0.0 24.4 jit_solution(14707460099226184109)
XLA Ops:
  0.6 22.1 %profits.1 = (f32[5,26,64]{2,1,0:T(8,128)}, f32[4,16,256]{2,1,0:T(8,128)}) custom-call(s32[3,12]{1,0:T(4,128)} %bitcast.13, s32[12]{0:T(128)} %bowner_in.1, s32[1,200]{1,0:T(1,128)} %bitcast.14, s32[8,1,1024]{2,1,0:T(1,128)} %bitcast.12, bf16[1000,1024]{1,0:T(8,128)(2,1)} %bitcast.9, bf16[64,1000]{1,0:T(8,128)(2,1)} %bitcast.11, bf16[200,1024]{1,0:T(8,128)(2,1)} %bitcast.10, ...), custom_call_target="tpu_custom_call" | custom-call | tf_op jit(solution)/shard_map/profits/pallas_call | solution.py:498
  22.7 1.6 %write_results.1 = (f32[5,26,64]{2,1,0:T(8,128)}, f32[5,26]{1,0:T(8,128)}, f32[1,26]{1,0:T(1,128)}) custom-call(f32[5,26,64]{2,1,0:T(8,128)} %get-tuple-element.8.profit, f32[4,16,256]{2,1,0:T(8,128)} %get-tuple-element.9.lists_in), custom_call_target="tpu_custom_call" | custom-call | tf_op jit(solution)/shard_map/write_results/pallas_call | solution.py:549

commit v8 on v7

--- a/solution.py
+++ b/solution.py
@@ -157,7 +157,7 @@
             )
         )
     ]
-    for copy in [load_reduced] + load_loadings + small:
+    for copy in [load_reduced] + load_loadings + small + [load_sensitivity] + load_gamma:
         copy.start()
 
     barrier = pltpu.get_barrier_semaphore()
@@ -219,9 +219,6 @@
     for i in range(PARTS):
         for copy in load_loadings[i * PIECES : (i + 1) * PIECES]:
             copy.wait()
-        if i == PARTS - 1:
-            for copy in [load_sensitivity] + load_gamma:
-                copy.start()
         win[REACH, i] = jnp.dot(
             rbuf[...], lbuf[:, columns(i)], preferred_element_type=F32
         ).astype(BF16)

time: 24.6 us -> 22.9 us (0.931)
  Pallas kernels: 23.7 us -> 22.1 us
    pallas_call x1, Pallas kernels: 22.1 us -> 20.5 us  [local_program(): pl.pallas_call(functools.partial(kernel, n, n_scen, desk_dev), out_shape=...]
where the time goes in v8:
time: 22.9 us; the launch traced here: 22.8 us
  Pallas kernels  22.1 us (97%)
  between operations  0.64 us (3%)
    pallas_call x1, Pallas kernels, local_program(): pl.pallas_call(functools.partial(kernel, n, n_scen, desk_dev), out_shape=...  20.5 us
    pallas_call x1, Pallas kernels, local_program(): pl.pallas_call(functools.partial(write_kernel, tail, desk_dev), out_shape...  1.64 us

profile of v8, /device:TPU:0, one launch (start us, length us, event | category | flops | bytes accessed | tf_op | source)
XLA Modules:
  0.0 22.8 jit_solution(11904546083487108680)
XLA Ops:
  0.6 20.5 %profits.1 = (f32[5,26,64]{2,1,0:T(8,128)}, f32[4,16,256]{2,1,0:T(8,128)}) custom-call(s32[3,12]{1,0:T(4,128)} %bitcast.13, s32[12]{0:T(128)} %bowner_in.1, s32[1,200]{1,0:T(1,128)} %bitcast.14, s32[8,1,1024]{2,1,0:T(1,128)} %bitcast.12, bf16[1000,1024]{1,0:T(8,128)(2,1)} %bitcast.9, bf16[64,1000]{1,0:T(8,128)(2,1)} %bitcast.11, bf16[200,1024]{1,0:T(8,128)(2,1)} %bitcast.10, ...), custom_call_target="tpu_custom_call" | custom-call | tf_op jit(solution)/shard_map/profits/pallas_call | solution.py:495
  21.1 1.6 %write_results.1 = (f32[5,26,64]{2,1,0:T(8,128)}, f32[5,26]{1,0:T(8,128)}, f32[1,26]{1,0:T(1,128)}) custom-call(f32[5,26,64]{2,1,0:T(8,128)} %get-tuple-element.8.profit, f32[4,16,256]{2,1,0:T(8,128)} %get-tuple-element.9.lists_in), custom_call_target="tpu_custom_call" | custom-call | tf_op jit(solution)/shard_map/write_results/pallas_call | solution.py:546
